TPU v7x, 256 devices: a whole 4x4x8 slice. The times are simulated.
256 devices in a mesh: grp: 8 (over x_hi, y), tp: 32 (over x_lo, z, core).
Axes of the slice: x: 4 (x_hi: 2, x_lo: 2; x = x_hi * 2 + x_lo), y: 4, z: 8, core: 2. Of those that a mesh axis runs over, the one named last changes fastest.
Arguments:
- tokens: bfloat16 [49152, 8192], P(('grp', 'tp')), may hold values from -30 to 30
- grad_up: bfloat16 [49152, 14336], P(('grp', 'tp')), may hold values from -24 to 24
- factor_down: float32 [32, 8192], P(None, 'grp'), may hold values from -6 to 6
- factor_up: float32 [14336, 32], P('tp'), may hold values from -18 to 18
- base_weight: bfloat16 [8192, 14336], P('grp', 'tp'), may hold values from -6 to 6
Outputs:
- new_down: float32 [32, 8192], P(None, 'grp')
- new_up: float32 [14336, 32], P('tp')
- merged: bfloat16 [8192, 14336], P('grp', 'tp')
All inputs are finite; a program needn't handle non-finite values.
Results may differ from a plain program's by a relative error of at most 0.0046.
The roundings to bfloat16 on the way count: a program that leaves them out, or rounds other values in their place, can miss the bound.
Values may be sent and summed in bfloat16 or wider, within the bound.
No kernel may reach another device: no remote copies, remote signals or barrier semaphores. Data moves between devices by JAX's collectives and lax.ppermute only.
A program may use at most 64 MiB of HBM per device.

v0:
```python
import jax
import jax.numpy as jnp
from jax import lax
from jax.sharding import PartitionSpec as P

adapter_scale = 0.25
step_size = 0.1
norm_eps = 1e-06


def shards(tokens, grad_up, factor_down, factor_up, base_weight):
    down_half = factor_down.astype(jnp.bfloat16)
    up_half = factor_up.astype(jnp.bfloat16)
    columns = tokens
    reduced = lax.dot_general(
        columns,
        lax.all_gather(down_half, "grp", axis=1, tiled=True),
        (((1,), (1,)), ((), ())),
        preferred_element_type=jnp.float32,
    ).astype(jnp.bfloat16)
    columns = grad_up
    returned = jnp.dot(
        columns,
        lax.all_gather(up_half, "tp", axis=0, tiled=True),
        preferred_element_type=jnp.float32,
    ).astype(jnp.bfloat16)
    grad_a_t = adapter_scale * lax.dot_general(
        tokens, returned, (((0,), (0,)), ((), ())), preferred_element_type=jnp.float32
    )
    grad_b = adapter_scale * lax.dot_general(
        grad_up, reduced, (((0,), (0,)), ((), ())), preferred_element_type=jnp.float32
    )
    owned_b, owned_a = (
        lax.psum_scatter(grad_b, ("grp", "tp"), scatter_dimension=0, tiled=True),
        lax.psum_scatter(grad_a_t, ("grp", "tp"), scatter_dimension=0, tiled=True),
    )
    local_gb = jnp.sum(owned_b * owned_b)
    local_ga = jnp.sum(owned_a * owned_a)
    local_pa = jnp.sum(factor_down * factor_down)
    local_pb = jnp.sum(factor_up * factor_up)
    squares_a, squares_b = lax.psum((local_ga, local_gb), ("grp", "tp"))
    param_a = lax.psum(local_pa, "grp")
    param_b = lax.psum(local_pb, "tp")
    slice_a = lax.all_gather(owned_a, "tp", axis=0, tiled=True)
    whole_b = lax.all_gather(owned_b, ("grp", "tp"), axis=0, tiled=True)
    height = factor_up.shape[0]
    slice_b = lax.dynamic_slice_in_dim(whole_b, lax.axis_index("tp") * height, height, 0)
    ratio_a = jnp.sqrt(param_a) / jnp.sqrt(squares_a + norm_eps)
    ratio_b = jnp.sqrt(param_b) / jnp.sqrt(squares_b + norm_eps)
    new_down = factor_down - step_size * ratio_a * slice_a.T
    new_up = factor_up - step_size * ratio_b * slice_b
    product = lax.dot_general(
        new_down.astype(jnp.bfloat16),
        new_up.astype(jnp.bfloat16),
        (((0,), (1,)), ((), ())),
        preferred_element_type=jnp.float32,
    )
    merged = (base_weight.astype(jnp.float32) + adapter_scale * product).astype(jnp.bfloat16)
    return (new_down, new_up, merged)


def solution(mesh):
    return jax.shard_map(
        shards,
        mesh=mesh,
        in_specs=(
            P(("grp", "tp"), None),
            P(("grp", "tp"), None),
            P(None, "grp"),
            P("tp", None),
            P("grp", "tp"),
        ),
        out_specs=(P(None, "grp"), P("tp", None), P("grp", "tp")),
        check_vma=False,
    )
```

profile of v0, /device:TPU:1, one launch (start us, length us, event | category | flops | bytes accessed | tf_op | source)
XLA Modules:
  0.0 2022.2 jit_solution(422413403181363957)
XLA Ops:
  7.2 1.8 fusion.4
  9.0 32.3 %all_gather.14 = bf16[32,8192]{1,0:T(8,128)(2,1)} all-gather(bf16[32,1024]{1,0:T(8,128)(2,1)S(1)} %get-tuple-element.10), channel_id=1, replica_groups=mesh['grp'=8,'tp'=32] {'grp'}, dimensions={1}, use_global_device_ids=true | all-gather | bytes 589824 | tf_op jit(solution)/shard_map/all_gather | solution.py:17
  41.4 7.2 fusion
  49.2 46.1 %all-gather = bf16[32,448,32]{1,2,0:T(8,128)(2,1)S(1)} all-gather(bf16[1,448,32]{1,2,0:T(8,128)(2,1)S(1)} %get-tuple-element.13), channel_id=1, replica_groups=mesh['grp'=8,'tp'=32] {'tp'}, dimensions={0}, use_global_device_ids=true | all-gather | bytes 946176 | tf_op jit(solution)/shard_map/all_gather | solution.py:24
  95.3 1.5 copy.10
  96.9 3.0 reshape.7
  99.9 7.0 fusion.1
  106.9 3.6 copy.15
  110.6 205.2 %all-reduce.4.cloned.1.call-done = f32[14336,32]{0,1:T(8,128)} async-done(((f32[14336,32]{0,1:T(8,128)}), f32[14336,32]{0,1:T(8,128)}) %all-reduce.4.cloned.1.call-update) | async-done | bytes 1835024
  315.8 2.0 dynamic-slice_bitcast_fusion
  317.8 55.1 %psum.30 = f32[]{:T(128)} all-reduce(f32[]{:T(128)} %get-tuple-element.12), channel_id=1, replica_groups=mesh['grp'=8,'tp'=32] {'tp'}, use_global_device_ids=true, to_apply=%region_6.0 | all-reduce | flops 1 | bytes 8 | tf_op jit(solution)/shard_map/psum | solution.py:43
  373.0 21.3 %psum.28 = f32[]{:T(128)} all-reduce(f32[]{:T(128)} %get-tuple-element.11), channel_id=1, replica_groups=mesh['grp'=8,'tp'=32] {'grp'}, use_global_device_ids=true, to_apply=%region_1.0 | all-reduce | flops 1 | bytes 8 | tf_op jit(solution)/shard_map/psum | solution.py:42
  394.2 1.0 copy.12
  396.5 1189.9 %reduce-scatter.5.cloned.1.call-done = f32[32,32]{1,0:T(8,128)} async-done(((f32[8192,32]{1,0:T(8,128)}), f32[32,32]{1,0:T(8,128)}) %reduce-scatter.5.cloned.1.call-update) | async-done | bytes 4112 | tf_op jit(solution)/shard_map/reduce_scatter | solution.py:35
  1586.4 0.8 copy.16
  1587.8 78.2 %all-reduce.1 = (f32[]{:T(128)}, f32[]{:T(128)}) all-reduce(f32[]{:T(128)} %multiply_reduce_fusion.3, f32[]{:T(128)} %get-tuple-element.9), channel_id=1, replica_groups=mesh['grp'=8,'tp'=32] {'grp','tp'}, use_global_device_ids=true, to_apply=%region_4.0 | all-reduce | flops 2 | bytes 16 | tf_op jit(solution)/shard_map/psum | solution.py:41
  1667.4 35.9 %all_gather.13 = f32[1024,32]{1,0:T(8,128)S(1)} all-gather(f32[32,32]{1,0:T(8,128)} %reduce-scatter.5.cloned.1.call-done), channel_id=1, replica_groups=mesh['grp'=8,'tp'=32] {'tp'}, dimensions={0}, use_global_device_ids=true | all-gather | bytes 135168 | tf_op jit(solution)/shard_map/all_gather | solution.py:44
  1703.3 1.9 bitcast_subtract_fusion
  1705.2 1.9 copy.14
  1707.1 292.9 %all-gather.4.cloned.1.call-done = f32[256,56,32]{1,2,0:T(8,128)} async-done(((f32[1,56,32]{1,2,0:T(8,128)}), f32[256,56,32]{1,2,0:T(8,128)}) %all-gather.4.cloned.1.call-update) | async-done | bytes 1835024 | tf_op jit(solution)/shard_map/all_gather | solution.py:45
  2000.0 6.6 copy.13
  2006.6 5.3 reshape.9
  2011.9 1.0 multiply_subtract_fusion
  2012.9 2.7 add_convert_fusion
  (16 shorter events, 1.4 us)
Async XLA Ops:
  7.2 34.2 %copy-start = (bf16[192,8192]{1,0:T(8,128)(2,1)S(1)}, bf16[192,8192]{1,0:T(8,128)(2,1)}, u32[]{:S(2)}) copy-start(bf16[192,8192]{1,0:T(8,128)(2,1)} %param.5) | copy-start | bytes 9437188
  7.2 308.6 %all-reduce.4.cloned.1.call-start = ((), (), s32[]{:S(2)}) async-start(), calls=%async_computation.3 | async-start | bytes 3670016
  41.4 7.2 copy-start.3
  48.5 1537.9 %reduce-scatter.5.cloned.1.call-start = ((), (), s32[]{:S(2)}) async-start(), calls=%async_computation.2 | async-start | bytes 4210688 | tf_op jit(solution)/shard_map/reduce_scatter | solution.py:35
  110.5 283.7 %copy-start.1 = (f32[32,1024]{1,0:T(8,128)S(1)}, f32[32,1024]{1,0:T(8,128)}, u32[]{:S(2)}) copy-start(f32[32,1024]{1,0:T(8,128)} %param.7) | copy-start | bytes 393220
  110.5 1889.5 %all-gather.4.cloned.1.call-start = ((), (), s32[]{:S(2)}) async-start(), calls=%async_computation.1 | async-start | bytes 4210688 | tf_op jit(solution)/shard_map/all_gather | solution.py:45
  2012.9 2.7 copy-start.2
Sparse Core Ops, SparseCore 0:
  48.7 267.0 all-reduce.3
  318.4 1267.9 reduce-scatter.4
  1588.9 411.0 all-gather.3
where the time goes:
time: 2020 us
  waiting for transfers between devices  1690 us (84%)
  blocking collectives  269 us (13%)
  local copies, waits for them, and re-layouts  23.8 us (1%)
    reduce_scatter x1, waiting for transfers between devices, shards(): lax.psum_scatter(grad_a_t, ('grp', 'tp'), scatter_dimension=0, tiled=True)  1190 us
    all_gather x1, waiting for transfers between devices, shards(): whole_b = lax.all_gather(owned_b, ('grp', 'tp'), axis=0, tiled=True)  293 us
    unnamed x4, waiting for transfers between devices  205 us
    psum x1, blocking collectives, shards(): squares_a, squares_b = lax.psum((local_ga, local_gb), ('grp', 'tp'))  78.2 us
    psum x1, blocking collectives, shards(): param_b = lax.psum(local_pb, 'tp')  55.1 us
    all_gather x1, blocking collectives, shards(): lax.all_gather(up_half, 'tp', axis=0, tiled=True)  46.1 us
  transfers between devices with their start and end apart: 3, of which 3 were waited for; matrix products, arithmetic and copies ran while one was open for 1% of the time, Pallas kernels for 0%

commit v1 on v0

v1 whole, which is shorter than its diff:
```python
import jax
import jax.numpy as jnp
from jax import lax
from jax.sharding import Mesh, PartitionSpec as P

adapter_scale = 0.25
step_size = 0.1
norm_eps = 1e-06

GRP = ("xh", "y")
TP = ("xl", "z", "c")
PLANE = ("xh", "y", "xl")
COLUMN = ("z", "c")


def spread(block, axes, count):
    return lax.all_to_all(
        jnp.broadcast_to(block[None], (count,) + block.shape), axes, 0, 0, tiled=True
    )


def shards(tokens, grad_up, factor_down, factor_up, base_weight):
    f32, bf16 = jnp.float32, jnp.bfloat16
    group = lax.axis_index(GRP)
    half = lax.axis_index("xl")
    core = lax.axis_index("c")

    down_half = lax.dynamic_slice_in_dim(factor_down.astype(bf16), core * 16, 16, 0)
    up_t = factor_up.T.astype(bf16)
    downs = spread(down_half, GRP, 8)
    ups = spread(up_t, ("xl", "z"), 16)
    downs = lax.all_gather(downs, "c", axis=0)
    ups = lax.all_gather(ups, "c", axis=1)
    down = downs.transpose(0, 2, 1, 3).reshape(32, 8192)
    up = ups.reshape(32, 32, 448).transpose(1, 0, 2).reshape(32, 14336)

    contract_last = (((1,), (1,)), ((), ()))
    contract_first = (((0,), (0,)), ((), ()))
    reduced = lax.dot_general(tokens, down, contract_last, preferred_element_type=f32).astype(bf16)
    returned = lax.dot_general(grad_up, up, contract_last, preferred_element_type=f32).astype(bf16)
    part_a = lax.dot_general(returned, tokens, contract_first, preferred_element_type=f32)
    part_b = lax.dot_general(reduced, grad_up, contract_first, preferred_element_type=f32)

    part_a = part_a.astype(bf16).reshape(2, 16, 8, 1024)
    part_b = part_b.astype(bf16).reshape(2, 16, 8, 1792)
    part = jnp.concatenate([part_a, part_b], 3).transpose(2, 0, 1, 3).reshape(16, 16, 2816)
    part = lax.all_to_all(part, PLANE, 0, 0, tiled=True)
    part = jnp.sum(part.astype(f32), axis=0).astype(bf16)
    part = lax.all_to_all(part.reshape(16, 22, 128), COLUMN, 0, 0, tiled=True)
    row = adapter_scale * jnp.sum(part.astype(f32), axis=0)
    squares = row * row
    sums = jnp.stack(
        [
            jnp.sum(squares[:8]),
            jnp.sum(squares[8:]),
            jnp.sum(factor_down * factor_down) * (1 / 32),
            jnp.sum(factor_up * factor_up) * (1 / 8),
        ]
    )

    row = jnp.concatenate([row, jnp.broadcast_to(sums[:, None], (4, 128)).reshape(4, 128)], 0)
    rows = spread(row, PLANE, 16).reshape(8, 2, 26, 128)
    sums = jnp.sum(rows[:, :, 22:], axis=(0, 1))
    row_a = lax.dynamic_index_in_dim(rows, group, 0, keepdims=False)[:, :8].reshape(2, 1024)
    row_b = lax.dynamic_slice_in_dim(rows[:, :, 8:22], half * 4, 4, 0)
    row_b = row_b.reshape(4, 2, 4, 448).transpose(0, 2, 1, 3).reshape(16, 2, 448)
    send = jnp.concatenate(
        [
            jnp.broadcast_to(row_a[None], (16, 2, 1024)),
            row_b,
            jnp.broadcast_to(sums[:, :16].reshape(1, 1, 64), (16, 2, 64)),
        ],
        2,
    )
    got = lax.all_to_all(send.reshape(16, 24, 128), COLUMN, 0, 0, tiled=True)
    got = got.reshape(16, 2, 1536).transpose(1, 0, 2).reshape(32, 1536)
    grad_a = got[:, :1024]
    grad_b = got[:, 1024:1472]
    sums = jnp.sum(got[:16, 1472:], axis=0).reshape(4, 16)[:, 0]

    ratio_a = jnp.sqrt(sums[2]) / jnp.sqrt(sums[0] + norm_eps)
    ratio_b = jnp.sqrt(sums[3]) / jnp.sqrt(sums[1] + norm_eps)
    new_down = factor_down - step_size * ratio_a * grad_a
    new_up = factor_up.T - step_size * ratio_b * grad_b
    product = lax.dot_general(
        new_down.astype(bf16), new_up.astype(bf16), contract_first, preferred_element_type=f32
    )
    merged = (base_weight.astype(f32) + adapter_scale * product).astype(bf16)
    return (new_down, new_up.T, merged)


def solution(mesh):
    fine = Mesh(mesh.devices.reshape(2, 4, 2, 8, 2), ("xh", "y", "xl", "z", "c"))
    return jax.shard_map(
        shards,
        mesh=fine,
        in_specs=(
            P(GRP + TP, None),
            P(GRP + TP, None),
            P(None, GRP),
            P(TP, None),
            P(GRP, TP),
        ),
        out_specs=(P(None, GRP), P(TP, None), P(GRP, TP)),
        check_vma=False,
    )
```

time: 2020 us -> 142 us (0.07)
  waiting for transfers between devices: 1690 us -> 21.3 us
  blocking collectives: 269 us -> 45.6 us
  starting transfers between devices: 0.12 us -> 27.2 us
    reduce_scatter x1 -> x0, waiting for transfers between devices: 1190 us -> none  [shards(): lax.psum_scatter(grad_a_t, ('grp', 'tp'), scatter_dimension=0, tiled=True)]
    all_gather x1 -> x0, waiting for transfers between devices: 293 us -> none  [shards(): whole_b = lax.all_gather(owned_b, ('grp', 'tp'), axis=0, tiled=True)]
    unnamed x4 -> x0, waiting for transfers between devices: 205 us -> none
    psum x3 -> x0, blocking collectives: 155 us -> none  [the longest x1 78.2 us: shards(): squares_a, squares_b = lax.psum((local_ga, local_gb), ('grp', 'tp'))]
    all_gather x3 -> x2, blocking collectives: 114 us -> 7.85 us  [the longest x1 4.19 us: shards(): downs = lax.all_gather(downs, 'c', axis=0)]
    all_to_all x0 -> x2, blocking collectives: none -> 37.7 us  [the longest x1 24 us: shards(): part = lax.all_to_all(part, PLANE, 0, 0, tiled=True)]
    all_to_all x0 -> x4, starting transfers between devices: none -> 27.2 us  [the longest x3 19.4 us: spread(): lax.all_to_all(jnp.broadcast_to(block[None], (count,) + block.shape), axe...]
    all_to_all x0 -> x4, waiting for transfers between devices: none -> 21.3 us  [the longest x3 14.7 us: spread(): lax.all_to_all(jnp.broadcast_to(block[None], (count,) + block.shape), axe...]
  transfers between devices with their start and end apart: 3 -> 4, of which waited for: 3 -> 3; matrix products, arithmetic and copies ran while one was open for 1% -> 9% of each run, Pallas kernels for 0% -> 0%
where the time goes in v1:
time: 142 us; the launch traced here: 141 us
  blocking collectives  45.6 us (32%)
  starting transfers between devices  27.2 us (19%)
  waiting for transfers between devices  21.3 us (15%)
  matrix products  16 us (11%)
  local copies, waits for them, and re-layouts  15.6 us (11%)
  other arithmetic  10.3 us (7%)
  between operations  4.94 us (3%)
    all_to_all x1, blocking collectives, shards(): part = lax.all_to_all(part, PLANE, 0, 0, tiled=True)  24 us
    all_to_all x3, starting transfers between devices, spread(): lax.all_to_all(jnp.broadcast_to(block[None], (count,) + block.shape), axe...  19.4 us
    all_to_all x3, waiting for transfers between devices, spread(): lax.all_to_all(jnp.broadcast_to(block[None], (count,) + block.shape), axe...  14.7 us
    all_to_all x1, blocking collectives, shards(): got = lax.all_to_all(send.reshape(16, 24, 128), COLUMN, 0, 0, tiled=True)  13.8 us
    all_to_all x1, starting transfers between devices, shards(): part = lax.all_to_all(part.reshape(16, 22, 128), COLUMN, 0, 0, tiled=True)  7.81 us
    dot_general x1, matrix products, shards(): lax.dot_general(reduced, grad_up, contract_first, preferred_element_type=...  6.83 us
    dot_general x1, matrix products, shards(): lax.dot_general(returned, tokens, contract_first, preferred_element_type=...  6.63 us
    all_to_all x1, waiting for transfers between devices, shards(): part = lax.all_to_all(part.reshape(16, 22, 128), COLUMN, 0, 0, tiled=True)  6.54 us
  transfers between devices with their start and end apart: 4, of which 3 were waited for; matrix products, arithmetic and copies ran while one was open for 9% of the time, Pallas kernels for 0%

profile of v1, /device:TPU:1, one launch (start us, length us, event | category | flops | bytes accessed | tf_op | source)
XLA Modules:
  0.0 141.0 jit_solution(14239816174384614577)
XLA Ops:
  2.4 7.5 %all-to-all-start.1 = ((bf16[8,16,1024]{2,1,0:T(8,128)(2,1)}), bf16[8,16,1024]{2,1,0:T(8,128)(2,1)S(1)}, u32[]{:S(2)}, u32[]{:S(2)}) async-start(bf16[8,16,1024]{2,1,0:T(8,128)(2,1)} %broadcast_in_dim.17), calls=%async_computation.1 | async-start | bytes 524288 | tf_op jit(solution)/shard_map/all_to_all | solution.py:17
  9.9 1.5 %multiply_reduce_fusion.1 = (f32[]{:T(128)}, bf16[32,448]{1,0:T(8,128)(2,1)S(1)}) fusion(f32[448,32]{0,1:T(8,128)} %param.8), kind=kLoop, calls=%fused_computation.15 | loop fusion | flops 43007 | bytes 86020 | tf_op jit(solution)/shard_map/reduce_sum | solution.py:57
  11.3 6.1 %all-to-all-done.1 = bf16[8,16,1024]{2,1,0:T(8,128)(2,1)S(1)} async-done(((bf16[8,16,1024]{2,1,0:T(8,128)(2,1)}), bf16[8,16,1024]{2,1,0:T(8,128)(2,1)S(1)}, u32[]{:S(2)}, u32[]{:S(2)}) %all-to-all-start.1) | async-done | bytes 262176 | tf_op jit(solution)/shard_map/all_to_all | solution.py:17
  18.3 8.4 %all-to-all-start = ((bf16[16,32,448]{2,1,0:T(8,128)(2,1)}), bf16[16,32,448]{2,1,0:T(8,128)(2,1)}, u32[]{:S(2)}, u32[]{:S(2)}) async-start(bf16[16,32,448]{2,1,0:T(8,128)(2,1)} %broadcast_in_dim.16), calls=%async_computation | async-start | bytes 1048576 | tf_op jit(solution)/shard_map/all_to_all | solution.py:17
  26.7 4.2 %all-gather.1 = bf16[16,16,1024]{2,1,0:T(8,128)(2,1)S(1)} all-gather(bf16[8,16,1024]{2,1,0:T(8,128)(2,1)S(1)} %all-to-all-done.1), channel_id=3, replica_groups=mesh['xh'=2,'y'=4,'xl'=2,'z'=8,'c'=2] {'c'}, dimensions={0}, use_global_device_ids=true | all-gather | bytes 786432 | tf_op jit(solution)/shard_map/all_gather | solution.py:32
  31.2 1.1 copy.24
  32.3 6.8 %convolution_convert_fusion = bf16[32,14336]{1,0:T(8,128)(2,1)} fusion(bf16[192,14336]{1,0:T(8,128)(2,1)} %param.6, bf16[32,8192]{1,0:T(8,128)(2,1)} %bitcast.57, bf16[192,8192]{1,0:T(8,128)(2,1)S(1)} %copy-done), kind=kOutput, calls=%fused_computation | convolution fusion | flops 277288960 | bytes 10092544 | tf_op jit(solution)/shard_map/dot_general | solution.py:42
  39.1 1.3 copy.25
  41.5 3.7 %all-gather = bf16[16,64,448]{2,1,0:T(8,128)(2,1)S(1)} all-gather(bf16[16,32,448]{2,1,0:T(8,128)(2,1)} %all-to-all-done), channel_id=2, replica_groups=mesh['xh'=2,'y'=4,'xl'=2,'z'=8,'c'=2] {'c'}, dimensions={1}, use_global_device_ids=true | all-gather | bytes 1376256 | tf_op jit(solution)/shard_map/all_gather | solution.py:33
  45.2 1.6 %copy.17 = bf16[32,32,448]{2,1,0:T(8,128)(2,1)} copy(bf16[32,32,448]{2,0,1:T(8,128)(2,1)S(1)} %bitcast.54) | data formatting | bytes 1835008 | tf_op jit(solution)/shard_map/transpose | solution.py:35
  46.7 3.0 %reshape.78 = bf16[32,14336]{1,0:T(8,128)(2,1)} reshape(bf16[32,32,448]{2,1,0:T(8,128)(2,1)} %copy.17) | data formatting | bytes 1835008 | tf_op jit(solution)/shard_map/reshape | solution.py:35
  49.7 6.6 %convolution_convert_fusion.1 = bf16[32,8192]{1,0:T(8,128)(2,1)} fusion(bf16[192,8192]{1,0:T(8,128)(2,1)S(1)} %copy-done, bf16[192,14336]{1,0:T(8,128)(2,1)} %param.6, bf16[32,14336]{1,0:T(8,128)(2,1)} %reshape.78), kind=kOutput, calls=%fused_computation.1 | convolution fusion | flops 277092352 | bytes 10092544 | tf_op jit(solution)/shard_map/dot_general | solution.py:41
  56.4 1.3 copy.23
  58.0 1.3 pad_maximum_fusion
  59.3 24.0 %all_to_all.30 = bf16[16,16,2816]{2,1,0:T(8,128)(2,1)} all-to-all(bf16[16,16,2816]{2,1,0:T(8,128)(2,1)S(1)} %bitcast.53), channel_id=1, replica_groups=mesh['xh'=2,'y'=4,'xl'=2,'z'=8,'c'=2] {'xh','y','xl'}, dimensions={0} | all-to-all | bytes 2883584 | tf_op jit(solution)/shard_map/all_to_all | solution.py:47
  83.3 1.6 %reduce_sum.75 = bf16[16,2816]{1,0:T(8,128)(2,1)S(1)} reduce(bf16[16,16,2816]{2,1,0:T(8,128)(2,1)} %all_to_all.30, bf16[]{:T(256)} %constant.15.clone.1), dimensions={0}, to_apply=%region_0.0 | reduce | flops 675840 | bytes 1531906 | tf_op jit(solution)/shard_map/reduce_sum | solution.py:48
  85.6 7.8 %all-to-all-start.3 = ((bf16[16,22,128]{2,1,0:T(8,128)(2,1)}), bf16[16,22,128]{2,1,0:T(8,128)(2,1)S(1)}, u32[]{:S(2)}, u32[]{:S(2)}) async-start(bf16[16,22,128]{2,1,0:T(8,128)(2,1)} %reshape.83), calls=%async_computation.3 | async-start | bytes 196608 | tf_op jit(solution)/shard_map/all_to_all | solution.py:49
  95.4 6.5 %all-to-all-done.3 = bf16[16,22,128]{2,1,0:T(8,128)(2,1)S(1)} async-done(((bf16[16,22,128]{2,1,0:T(8,128)(2,1)}), bf16[16,22,128]{2,1,0:T(8,128)(2,1)S(1)}, u32[]{:S(2)}, u32[]{:S(2)}) %all-to-all-start.3) | async-done | bytes 90144 | tf_op jit(solution)/shard_map/all_to_all | solution.py:49
  103.2 1.4 pad_maximum_fusion.2
  105.4 3.5 %all-to-all-start.4 = ((f32[16,26,128]{2,1,0:T(8,128)}), f32[16,26,128]{2,1,0:T(8,128)S(1)}, u32[]{:S(2)}, u32[]{:S(2)}) async-start(f32[16,26,128]{2,1,0:T(8,128)} %broadcast_in_dim.19), calls=%async_computation.4 | async-start | bytes 524288 | tf_op jit(solution)/shard_map/all_to_all | solution.py:17
  109.0 8.6 %all-to-all-done.4 = f32[16,26,128]{2,1,0:T(8,128)S(1)} async-done(((f32[16,26,128]{2,1,0:T(8,128)}), f32[16,26,128]{2,1,0:T(8,128)S(1)}, u32[]{:S(2)}, u32[]{:S(2)}) %all-to-all-start.4) | async-done | bytes 213024 | tf_op jit(solution)/shard_map/all_to_all | solution.py:17
  118.4 13.8 %all_to_all.31 = f32[16,24,128]{2,1,0:T(8,128)S(1)} all-to-all(f32[16,24,128]{2,1,0:T(8,128)S(1)} %reshape.87), channel_id=1, replica_groups=mesh['xh'=2,'y'=4,'xl'=2,'z'=8,'c'=2] {'z','c'}, dimensions={0} | all-to-all | bytes 393216 | tf_op jit(solution)/shard_map/all_to_all | solution.py:75
  136.8 1.5 %fusion.5 = f32[448,32]{0,1:T(8,128)} fusion(f32[32,1536]{1,0:T(8,128)S(1)} %bitcast.64, f32[]{:T(128)} %bitcast.18, f32[448,32]{0,1:T(8,128)} %param.8), kind=kLoop, calls=%fused_computation.19 | loop fusion | flops 28672 | bytes 172036 | tf_op jit(solution)/shard_map/transpose | solution.py:89
  138.4 2.6 %add_convert_fusion = bf16[1024,448]{0,1:T(8,128)(2,1)} fusion(bf16[1024,448]{0,1:T(8,128)(2,1)} %param.9, f32[32,1024]{1,0:T(8,128)S(1)} %fusion, f32[32,1536]{1,0:T(8,128)S(1)} %bitcast.65, f32[448,32]{0,1:T(8,128)} %param.8, f32[]{:T(128)} %bitcast.18), kind=kOutput, calls=%fused_computation.2 | convolution fusion | flops 31270912 | bytes 2088964 | tf_op jit(solution)/shard_map/dot_general | solution.py:85
  (40 shorter events, 10.3 us)
Async XLA Ops:
  0.6 31.7 %copy-start = (bf16[192,8192]{1,0:T(8,128)(2,1)S(1)}, bf16[192,8192]{1,0:T(8,128)(2,1)}, u32[]{:S(2)}) copy-start(bf16[192,8192]{1,0:T(8,128)(2,1)} %param.5) | copy-start | bytes 9437188
  2.4 15.1 %all-to-all-start.1 = ((bf16[8,16,1024]{2,1,0:T(8,128)(2,1)}), bf16[8,16,1024]{2,1,0:T(8,128)(2,1)S(1)}, u32[]{:S(2)}, u32[]{:S(2)}) async-start(bf16[8,16,1024]{2,1,0:T(8,128)(2,1)} %broadcast_in_dim.17), calls=%async_computation.1 | async-start | bytes 524288 | tf_op jit(solution)/shard_map/all_to_all | solution.py:17
  18.3 23.2 %all-to-all-start = ((bf16[16,32,448]{2,1,0:T(8,128)(2,1)}), bf16[16,32,448]{2,1,0:T(8,128)(2,1)}, u32[]{:S(2)}, u32[]{:S(2)}) async-start(bf16[16,32,448]{2,1,0:T(8,128)(2,1)} %broadcast_in_dim.16), calls=%async_computation | async-start | bytes 1048576 | tf_op jit(solution)/shard_map/all_to_all | solution.py:17
  58.0 36.0 %copy-start.1 = (f32[32,1024]{1,0:T(8,128)S(1)}, f32[32,1024]{1,0:T(8,128)}, u32[]{:S(2)}) copy-start(f32[32,1024]{1,0:T(8,128)} %param.7) | copy-start | bytes 393220
  85.6 16.3 %all-to-all-start.3 = ((bf16[16,22,128]{2,1,0:T(8,128)(2,1)}), bf16[16,22,128]{2,1,0:T(8,128)(2,1)S(1)}, u32[]{:S(2)}, u32[]{:S(2)}) async-start(bf16[16,22,128]{2,1,0:T(8,128)(2,1)} %reshape.83), calls=%async_computation.3 | async-start | bytes 196608 | tf_op jit(solution)/shard_map/all_to_all | solution.py:49
  105.4 12.1 %all-to-all-start.4 = ((f32[16,26,128]{2,1,0:T(8,128)}), f32[16,26,128]{2,1,0:T(8,128)S(1)}, u32[]{:S(2)}, u32[]{:S(2)}) async-start(f32[16,26,128]{2,1,0:T(8,128)} %broadcast_in_dim.19), calls=%async_computation.4 | async-start | bytes 524288 | tf_op jit(solution)/shard_map/all_to_all | solution.py:17
  136.8 4.1 %copy-start.2 = (f32[32,1024]{1,0:T(8,128)}, f32[32,1024]{1,0:T(8,128)S(1)}, u32[]{:S(2)}) copy-start(f32[32,1024]{1,0:T(8,128)S(1)} %fusion) | copy-start | bytes 393220

commit v2 on v1

v2 whole, which is shorter than its diff:
```python
import jax
import jax.numpy as jnp
from jax import lax
from jax.experimental import pallas as pl
from jax.experimental.pallas import tpu as pltpu
from jax.sharding import Mesh, PartitionSpec as P

adapter_scale = 0.25
step_size = 0.1
norm_eps = 1e-06

GRP = ("xh", "y")
TP = ("xl", "z", "c")
PLANE = ("xh", "y", "xl")
COLUMN = ("z", "c")
f32, bf16 = jnp.float32, jnp.bfloat16
ALONG_LANES = (((1,), (1,)), ((), ()))
VMEM = pl.BlockSpec(memory_space=pltpu.VMEM)
SMEM = pl.BlockSpec(memory_space=pltpu.SMEM)
HBM = pl.BlockSpec(memory_space=pltpu.HBM)


def in_vmem(x):
    return pltpu.with_memory_space_constraint(x, pltpu.VMEM)


def in_hbm(x):
    return pltpu.with_memory_space_constraint(x, pltpu.HBM)


def exchange(x, axes):
    return lax.all_to_all(x, axes, 0, 0, tiled=True)


def load_kernel(tokens_hbm, grads_hbm, factor_down, factor_up, tokens, grads, norms, sems):
    copies = []
    for n, (source, target) in enumerate(((tokens_hbm, tokens), (grads_hbm, grads))):
        for k in range(4):
            rows = pl.ds(48 * k, 48)
            copies.append(pltpu.make_async_copy(source.at[rows], target.at[rows], sems.at[4 * n + k]))
    for copy in copies:
        copy.start()
    down, up = factor_down[...], factor_up[...]
    norms[...] = jnp.zeros((8, 128), f32)
    norms[0:1] = jnp.full((1, 128), jnp.sum(down * down) * (1 / 4096), f32)
    norms[1:2] = jnp.full((1, 128), jnp.sum(up * up) * (1 / 1024), f32)
    for copy in copies:
        copy.wait()


def gradients_kernel(
    place, tokens, grads, down0, down1, down2, down3, ups, ups_other, out
):
    owned = []
    for ky, blocks in enumerate((down0, down1, down2, down3)):
        for kx in range(2):
            owner = (place[0] ^ kx) * 4 + (place[1] ^ ky)
            columns = pl.ds(pl.multiple_of(owner * 1024, 1024), 1024)
            owned.append((columns, blocks, kx))
    reduced = jnp.zeros((192, 32), f32)
    for n, (columns, blocks, kx) in enumerate(owned):
        reduced += lax.dot_general(
            tokens[:, columns], blocks[kx], ALONG_LANES, preferred_element_type=f32
        )
    reduced_t = reduced.T.astype(bf16)
    returned = jnp.zeros((192, 32), f32)
    for pair in range(16):
        for other, blocks in enumerate((ups, ups_other)):
            start = pair * 896 + (place[3] ^ other) * 384
            columns = pl.ds(pl.multiple_of(start, 128), 512)
            returned += lax.dot_general(
                grads[:, columns], blocks[pair], ALONG_LANES, preferred_element_type=f32
            )
    returned_t = returned.T.astype(bf16)
    for g in range(8):
        part_b = jnp.dot(reduced_t, grads[:, g * 1792 : (g + 1) * 1792], preferred_element_type=f32)
        part_a = jnp.dot(returned_t, tokens[:, g * 1024 : (g + 1) * 1024], preferred_element_type=f32)
        for h in range(2):
            out[2 * g + h, :, :1024] = part_a[16 * h : 16 * h + 16].astype(bf16)
            out[2 * g + h, :, 1024:] = part_b[16 * h : 16 * h + 16].astype(bf16)


def plane_sum_kernel(parts, out, rows):
    for j in range(22):
        columns = slice(128 * j, 128 * j + 128)
        total = parts[0, :, columns].astype(f32)
        for k in range(1, 16):
            total += parts[k, :, columns].astype(f32)
        for h in range(2):
            rows[pl.ds(8 * h * 25 + j, 8, 25), :] = total[8 * h : 8 * h + 8]
    for r in range(16):
        out[r] = rows[pl.ds(r * 25, 22), :].astype(bf16)


def column_sum_kernel(norms, parts, out, rows):
    total = parts[0].astype(f32)
    for k in range(1, 16):
        total += parts[k].astype(f32)
    total = adapter_scale * total
    squares = total * total
    rows[...] = jnp.zeros((32, 128), f32)
    rows[pl.ds(0, 22), :] = total
    sums = (
        jnp.sum(squares[:8], axis=0, keepdims=True),
        jnp.sum(squares[8:], axis=0, keepdims=True),
        norms[0:1],
        norms[1:2],
    )
    for k, line in enumerate(sums):
        high = line.astype(bf16).astype(f32)
        rows[pl.ds(24 + k, 1), :] = high
        rows[pl.ds(28 + k, 1), :] = line - high
    block = rows[...].astype(bf16)
    for k in range(16):
        out[k] = block


def reroute_kernel(place, parts, out, rows):
    group, half = place[0] * 4 + place[1], place[2]
    sums = jnp.zeros((4, 128), f32)
    for g in range(8):
        for h in range(2):
            block = parts[2 * g + h].astype(f32)
            sums += block[24:28] + block[28:32]
    high = sums.astype(bf16).astype(f32)
    low = sums - high
    for h in range(2):
        mine = parts[2 * group + h].astype(f32)[:8]
        for section in range(4):
            block = parts[2 * (half * 4 + section) + h].astype(f32)
            for odd in range(2):
                for core in range(2):
                    start = 8 + 7 * odd + 3 * core
                    rows[(2 * section + odd) * 2 + core, pl.ds(16 * h, 8), :] = mine
                    rows[(2 * section + odd) * 2 + core, pl.ds(16 * h + 8, 4), :] = block[start : start + 4]
                    rows[(2 * section + odd) * 2 + core, pl.ds(16 * h + 12, 4), :] = low if h else high
    for k in range(16):
        out[k] = rows[k].astype(bf16)


def update_kernel(place, parts, factor_down, factor_up, base, new_down, new_up, merged, rows):
    sums = jnp.zeros((4, 128), f32)
    for k in range(16):
        block = parts[k].astype(f32)
        rows[pl.ds(k * 33, 32), :] = block
        sums += block[12:16] + block[28:32]
    sums = jnp.sum(sums, axis=1, keepdims=True)
    scale_a = step_size * jnp.sqrt(sums[2:3]) / jnp.sqrt(sums[0:1] + norm_eps)
    scale_b = step_size * jnp.sqrt(sums[3:4]) / jnp.sqrt(sums[1:2] + norm_eps)

    def ranks(j):
        tiles = [rows[pl.ds(8 * q * 33 + 16 * h + j, 8, 33), :] for h in range(2) for q in range(2)]
        return jnp.concatenate(tiles, 0)

    for j in range(8):
        columns = slice(128 * j, 128 * j + 128)
        new_down[:, columns] = factor_down[:, columns] - scale_a * ranks(j)
    grad_b = jnp.concatenate([ranks(8 + j) for j in range(4)], 1)
    grad_b = jnp.where(place[3] == 0, grad_b, pltpu.roll(grad_b, 448, 1))[:, :448]
    new_up[...] = factor_up[...] - scale_b * grad_b
    left = new_up[...].T.astype(bf16)
    right = new_down[...].astype(bf16)
    for k in range(7):
        lines = slice(64 * k, 64 * k + 64)
        product = jnp.dot(left[lines], right, preferred_element_type=f32)
        merged[lines] = (base[lines].astype(f32) + adapter_scale * product).astype(bf16)


def shards(tokens, grad_up, factor_down, factor_up, base_weight):
    place = jnp.stack([lax.axis_index(name) for name in ("xh", "y", "xl", "c")]).astype(jnp.int32)
    factor_up = factor_up.T

    up = factor_up.astype(bf16)
    up = jnp.where(place[3] == 0, jnp.pad(up, ((0, 0), (0, 64))), jnp.pad(up, ((0, 0), (64, 0))))
    ups = exchange(jnp.broadcast_to(up[None], (16, 32, 512)), ("xl", "z"))
    down = factor_down.astype(bf16)
    down0 = jnp.stack([down, lax.ppermute(down, "xh", [(0, 1), (1, 0)])])
    downs = [down0] + [lax.ppermute(down0, "y", [(i, i ^ k) for i in range(4)]) for k in (1, 2, 3)]
    ups, downs = lax.optimization_barrier((ups, downs))
    ups_other = lax.ppermute(ups, "c", [(0, 1), (1, 0)])
    tokens, grad_up, norms = pl.pallas_call(
        load_kernel,
        out_shape=(
            pltpu.VMEM((192, 8192), bf16),
            pltpu.VMEM((192, 14336), bf16),
            jax.ShapeDtypeStruct((8, 128), f32),
        ),
        in_specs=[HBM, HBM, VMEM, VMEM],
        out_specs=(VMEM, VMEM, VMEM),
        scratch_shapes=[pltpu.SemaphoreType.DMA((8,))],
        compiler_params=pltpu.CompilerParams(vmem_limit_bytes=16 * 1024 * 1024),
        cost_estimate=pl.CostEstimate(flops=0, bytes_accessed=17 * 1024 * 1024, transcendentals=0),
        name="load",
    )(in_hbm(tokens), in_hbm(grad_up), factor_down, factor_up)
    params = pltpu.CompilerParams(vmem_limit_bytes=24 * 1024 * 1024)
    parts = pl.pallas_call(
        gradients_kernel,
        out_shape=jax.ShapeDtypeStruct((16, 16, 2816), bf16),
        in_specs=[SMEM] + [VMEM] * 8,
        out_specs=VMEM,
        compiler_params=params,
        name="gradients",
    )(place, tokens, grad_up, *downs, ups, ups_other)
    parts = in_vmem(exchange(parts, PLANE))
    parts = pl.pallas_call(
        plane_sum_kernel,
        out_shape=jax.ShapeDtypeStruct((16, 22, 128), bf16),
        in_specs=[VMEM],
        out_specs=VMEM,
        scratch_shapes=[pltpu.VMEM((400, 128), f32)],
        name="plane_sum",
    )(parts)
    parts = in_vmem(exchange(parts, COLUMN))
    parts = pl.pallas_call(
        column_sum_kernel,
        out_shape=jax.ShapeDtypeStruct((16, 32, 128), bf16),
        in_specs=[VMEM, VMEM],
        out_specs=VMEM,
        scratch_shapes=[pltpu.VMEM((32, 128), f32)],
        name="column_sum",
    )(norms, parts)
    parts = in_vmem(exchange(parts, PLANE))
    parts = pl.pallas_call(
        reroute_kernel,
        out_shape=jax.ShapeDtypeStruct((16, 32, 128), bf16),
        in_specs=[SMEM, VMEM],
        out_specs=VMEM,
        scratch_shapes=[pltpu.VMEM((16, 32, 128), f32)],
        name="reroute",
    )(place, parts)
    parts = in_vmem(exchange(parts, COLUMN))
    new_down, new_up, merged = pl.pallas_call(
        update_kernel,
        out_shape=(
            jax.ShapeDtypeStruct((32, 1024), f32),
            jax.ShapeDtypeStruct((32, 448), f32),
            jax.ShapeDtypeStruct((448, 1024), bf16),
        ),
        in_specs=[SMEM] + [VMEM] * 4,
        out_specs=(VMEM, VMEM, VMEM),
        scratch_shapes=[pltpu.VMEM((528, 128), f32)],
        name="update",
    )(place, parts, factor_down, factor_up, base_weight.T)
    return (new_down, new_up.T, merged.T)


def solution(mesh):
    fine = Mesh(mesh.devices.reshape(2, 4, 2, 8, 2), ("xh", "y", "xl", "z", "c"))
    return jax.shard_map(
        shards,
        mesh=fine,
        in_specs=(
            P(GRP + TP, None),
            P(GRP + TP, None),
            P(None, GRP),
            P(TP, None),
            P(GRP, TP),
        ),
        out_specs=(P(None, GRP), P(TP, None), P(GRP, TP)),
        check_vma=False,
    )
```

time: 142 us -> 117 us (0.82)
  blocking collectives: 45.6 us -> 67.2 us
  matrix products: 16 us -> 0 us
  Pallas kernels: 0 us -> 16 us
  waiting for transfers between devices: 21.3 us -> 7.24 us
  local copies, waits for them, and re-layouts: 15.6 us -> 2.6 us
  other arithmetic: 10.3 us -> 2.85 us
  starting transfers between devices: 27.2 us -> 19.8 us
  between operations: 4.94 us -> 0.7 us
    all_to_all x2 -> x4, blocking collectives: 37.7 us -> 67.2 us  [exchange(): return lax.all_to_all(x, axes, 0, 0, tiled=True)]
    all_to_all x4 -> x1, waiting for transfers between devices: 21.3 us -> 0.01 us  [exchange(): return lax.all_to_all(x, axes, 0, 0, tiled=True)]
    all_to_all x4 -> x1, starting transfers between devices: 27.2 us -> 10 us  [exchange(): return lax.all_to_all(x, axes, 0, 0, tiled=True)]
    dot_general x3 -> x0, matrix products: 16 us -> none  [the longest x1 6.83 us: shards(): lax.dot_general(reduced, grad_up, contract_first, preferred_element_type=...]
    pallas_call x0 -> x6, Pallas kernels: none -> 16 us  [the longest x1 6 us: shards(): pl.pallas_call(gradients_kernel, out_shape=jax.ShapeDtypeStruct((16, 16,...]
    ppermute x0 -> x5, starting transfers between devices: none -> 9.73 us  [the longest x3 4.01 us: shards(): lax.ppermute(down0, 'y', [(i, i ^ k) for i in range(4)])]
    all_gather x2 -> x0, blocking collectives: 7.85 us -> none  [the longest x1 4.19 us: shards(): downs = lax.all_gather(downs, 'c', axis=0)]
    ppermute x0 -> x5, waiting for transfers between devices: none -> 7.24 us  [the longest x3 5.55 us: shards(): lax.ppermute(down0, 'y', [(i, i ^ k) for i in range(4)])]
  transfers between devices with their start and end apart: 4 -> 6, of which waited for: 3 -> 4; matrix products, arithmetic and copies ran while one was open for 9% -> 2% of each run, Pallas kernels for 0% -> 3%
where the time goes in v2:
time: 117 us; the launch traced here: 116 us
  blocking collectives  67.2 us (57%)
  starting transfers between devices  19.8 us (17%)
  Pallas kernels  16 us (14%)
  waiting for transfers between devices  7.24 us (6%)
  other arithmetic  2.85 us (2%)
  local copies, waits for them, and re-layouts  2.6 us (2%)
    all_to_all x4, blocking collectives, exchange(): return lax.all_to_all(x, axes, 0, 0, tiled=True)  67.2 us
    all_to_all x1, starting transfers between devices, exchange(): return lax.all_to_all(x, axes, 0, 0, tiled=True)  10 us
    pallas_call x1, Pallas kernels, shards(): pl.pallas_call(gradients_kernel, out_shape=jax.ShapeDtypeStruct((16, 16,...  6 us
    ppermute x3, waiting for transfers between devices, shards(): lax.ppermute(down0, 'y', [(i, i ^ k) for i in range(4)])  5.55 us
    ppermute x3, starting transfers between devices, shards(): lax.ppermute(down0, 'y', [(i, i ^ k) for i in range(4)])  4.01 us
    pallas_call x1, Pallas kernels, shards(): pl.pallas_call(load_kernel, out_shape=(pltpu.VMEM((192, 8192), bf16), plt...  3.58 us
    ppermute x1, starting transfers between devices, shards(): ups_other = lax.ppermute(ups, 'c', [(0, 1), (1, 0)])  3.19 us
    pallas_call x1, Pallas kernels, shards(): pl.pallas_call(update_kernel, out_shape=(jax.ShapeDtypeStruct((32, 1024),...  2.83 us
  transfers between devices with their start and end apart: 6, of which 4 were waited for; matrix products, arithmetic and copies ran while one was open for 2% of the time, Pallas kernels for 3%

profile of v2, /device:TPU:1, one launch (start us, length us, event | category | flops | bytes accessed | tf_op | source)
XLA Modules:
  0.0 116.3 jit_solution(16832611317063230249)
XLA Ops:
  0.6 0.8 bitcast_convert_fusion
  1.6 0.8 broadcast_in_dim.2
  2.4 10.0 %all-to-all-start = ((bf16[16,32,512]{2,1,0:T(8,128)(2,1)}), bf16[16,32,512]{2,1,0:T(8,128)(2,1)S(1)}, u32[]{:S(2)}, u32[]{:S(2)}) async-start(bf16[16,32,512]{2,1,0:T(8,128)(2,1)} %broadcast_in_dim.2), calls=%async_computation | async-start | bytes 1048576 | tf_op jit(solution)/shard_map/all_to_all | solution.py:32
  12.5 0.9 convert_element_type.11
  13.4 2.5 %collective-permute-start = (bf16[32,1024]{1,0:T(8,128)(2,1)S(1)}, bf16[32,1024]{1,0:T(8,128)(2,1)S(1)}, u32[]{:S(2)}, u32[]{:S(2)}) collective-permute-start(bf16[32,1024]{1,0:T(8,128)(2,1)S(1)} %convert_element_type.11), channel_id=1, source_target_pairs={{0,128},{128,0},{1,129},{129,1},{2,130},{130,2},{3,131},{131,3},{4... | collective-permute-start | bytes 196616 | tf_op jit(solution)/shard_map/ppermute | solution.py:177
  15.9 0.9 convert_bitcast_fusion
  16.8 1.7 %collective-permute-done = bf16[32,1024]{1,0:T(8,128)(2,1)S(1)} collective-permute-done((bf16[32,1024]{1,0:T(8,128)(2,1)S(1)}, bf16[32,1024]{1,0:T(8,128)(2,1)S(1)}, u32[]{:S(2)}, u32[]{:S(2)}) %collective-permute-start) | collective-permute-done | bytes 65568 | tf_op jit(solution)/shard_map/ppermute | solution.py:177
  18.5 1.4 %collective-permute-start.1 = (bf16[2,32,1024]{2,1,0:T(8,128)(2,1)S(1)}, bf16[2,32,1024]{2,1,0:T(8,128)(2,1)S(1)}, u32[]{:S(2)}, u32[]{:S(2)}) collective-permute-start(bf16[2,32,1024]{2,1,0:T(8,128)(2,1)S(1)} %pad_maximum_fusion.down0), channel_id=1, source_target_pairs={{0,32},{32,0},{64,96},{96,64},{1,33},{33,1},{65,97},{97,65},{2,34}... | collective-permute-start | bytes 393224 | tf_op jit(solution)/shard_map/ppermute | solution.py:178
  19.9 2.6 %collective-permute-start.2 = (bf16[2,32,1024]{2,1,0:T(8,128)(2,1)S(1)}, bf16[2,32,1024]{2,1,0:T(8,128)(2,1)S(1)}, u32[]{:S(2)}, u32[]{:S(2)}) collective-permute-start(bf16[2,32,1024]{2,1,0:T(8,128)(2,1)S(1)} %pad_maximum_fusion.down0), channel_id=1, source_target_pairs={{0,64},{32,96},{64,0},{96,32},{1,65},{33,97},{65,1},{97,33},{2,66}... | collective-permute-start | bytes 393224 | tf_op jit(solution)/shard_map/ppermute | solution.py:178
  22.7 4.2 %collective-permute-done.2.down2 = bf16[2,32,1024]{2,1,0:T(8,128)(2,1)S(1)} collective-permute-done((bf16[2,32,1024]{2,1,0:T(8,128)(2,1)S(1)}, bf16[2,32,1024]{2,1,0:T(8,128)(2,1)S(1)}, u32[]{:S(2)}, u32[]{:S(2)}) %collective-permute-start.2) | collective-permute-done | bytes 131104 | tf_op jit(solution)/shard_map/ppermute | solution.py:178
  26.9 1.2 %collective-permute-done.3.down3 = bf16[2,32,1024]{2,1,0:T(8,128)(2,1)S(1)} collective-permute-done((bf16[2,32,1024]{2,1,0:T(8,128)(2,1)S(1)}, bf16[2,32,1024]{2,1,0:T(8,128)(2,1)S(1)}, u32[]{:S(2)}, u32[]{:S(2)}) %collective-permute-start.3) | collective-permute-done | bytes 131104 | tf_op jit(solution)/shard_map/ppermute | solution.py:178
  28.1 3.2 %collective-permute-start.4 = (bf16[16,32,512]{2,1,0:T(8,128)(2,1)S(1)}, bf16[16,32,512]{2,1,0:T(8,128)(2,1)S(1)}, u32[]{:S(2)}, u32[]{:S(2)}) collective-permute-start(bf16[16,32,512]{2,1,0:T(8,128)(2,1)S(1)} %all-to-all-done.ups), channel_id=1, source_target_pairs={{0,1},{1,0},{2,3},{3,2},{4,5},{5,4},{6,7},{7,6},{8,9},{9,8},{10,11... | collective-permute-start | bytes 1572872 | tf_op jit(solution)/shard_map/ppermute | solution.py:180
  31.3 0.9 copy-done
  32.2 0.8 copy-done.1
  33.0 3.6 %load.1 = (bf16[192,8192]{1,0:T(8,128)(2,1)S(1)}, bf16[192,14336]{1,0:T(8,128)(2,1)S(1)}, f32[8,128]{1,0:T(8,128)S(1)}) custom-call(bf16[192,8192]{1,0:T(8,128)(2,1)} %tokens_hbm.1, bf16[192,14336]{1,0:T(8,128)(2,1)} %grads_hbm.1, f32[32,1024]{1,0:T(8,128)S(1)} %copy-done, f32[32,448]{1,0:T(8,128)S(1)} %bitcast.13), custom_call_target="tpu_custom_call" | custom-call | bytes 17825792 | tf_op jit(solution)/shard_map/load/pallas_call | solution.py:181
  36.7 6.0 %gradients.1 = bf16[16,16,2816]{2,1,0:T(8,128)(2,1)S(1)} custom-call(s32[4]{0:T(128)S(1)} %pad_add_fusion.place, bf16[192,8192]{1,0:T(8,128)(2,1)S(1)} %get-tuple-element.15.tokens, bf16[192,14336]{1,0:T(8,128)(2,1)S(1)} %get-tuple-element.16.grads, bf16[2,32,1024]{2,1,0:T(8,128)(2,1)S(1)} %pad_maximum_fusion.down0, ...), custom_call_target="tpu_custom_call" | custom-call | tf_op jit(solution)/shard_map/gradients/pallas_call | solution.py:196
  42.7 26.9 %all_to_all.25.parts = bf16[16,16,2816]{2,1,0:T(8,128)(2,1)S(1)} all-to-all(bf16[16,16,2816]{2,1,0:T(8,128)(2,1)S(1)} %gradients.1), channel_id=1, replica_groups=mesh['xh'=2,'y'=4,'xl'=2,'z'=8,'c'=2] {'xh','y','xl'}, dimensions={0} | all-to-all | bytes 2883584 | tf_op jit(solution)/shard_map/all_to_all | solution.py:32
  69.7 0.8 plane_sum.1
  70.5 16.1 %all_to_all.26.parts = bf16[16,22,128]{2,1,0:T(8,128)(2,1)S(1)} all-to-all(bf16[16,22,128]{2,1,0:T(8,128)(2,1)} %plane_sum.1), channel_id=1, replica_groups=mesh['xh'=2,'y'=4,'xl'=2,'z'=8,'c'=2] {'z','c'}, dimensions={0} | all-to-all | bytes 180224 | tf_op jit(solution)/shard_map/all_to_all | solution.py:32
  86.6 1.4 %column_sum.1 = bf16[16,32,128]{2,1,0:T(8,128)(2,1)} custom-call(f32[8,128]{1,0:T(8,128)} %copy-done.3, bf16[16,22,128]{2,1,0:T(8,128)(2,1)S(1)} %all_to_all.26.parts), custom_call_target="tpu_custom_call" | custom-call | tf_op jit(solution)/shard_map/column_sum/pallas_call | solution.py:214
  88.0 10.9 %all_to_all.27.parts = bf16[16,32,128]{2,1,0:T(8,128)(2,1)S(1)} all-to-all(bf16[16,32,128]{2,1,0:T(8,128)(2,1)} %column_sum.1), channel_id=1, replica_groups=mesh['xh'=2,'y'=4,'xl'=2,'z'=8,'c'=2] {'xh','y','xl'}, dimensions={0} | all-to-all | bytes 262144 | tf_op jit(solution)/shard_map/all_to_all | solution.py:32
  98.8 1.4 %reroute.1 = bf16[16,32,128]{2,1,0:T(8,128)(2,1)} custom-call(s32[4]{0:T(128)} %copy-done.2, bf16[16,32,128]{2,1,0:T(8,128)(2,1)S(1)} %all_to_all.27.parts), custom_call_target="tpu_custom_call" | custom-call | tf_op jit(solution)/shard_map/reroute/pallas_call | solution.py:223
  100.2 13.3 %all_to_all.28.parts = bf16[16,32,128]{2,1,0:T(8,128)(2,1)S(1)} all-to-all(bf16[16,32,128]{2,1,0:T(8,128)(2,1)} %reroute.1), channel_id=1, replica_groups=mesh['xh'=2,'y'=4,'xl'=2,'z'=8,'c'=2] {'z','c'}, dimensions={0} | all-to-all | bytes 262144 | tf_op jit(solution)/shard_map/all_to_all | solution.py:32
  113.5 2.8 %update.1 = (f32[32,1024]{1,0:T(8,128)}, f32[32,448]{1,0:T(8,128)}, bf16[448,1024]{1,0:T(8,128)(2,1)}) custom-call(s32[4]{0:T(128)} %copy-done.2, bf16[16,32,128]{2,1,0:T(8,128)(2,1)S(1)} %all_to_all.28.parts, f32[32,1024]{1,0:T(8,128)} %factor_down.3, f32[32,448]{1,0:T(8,128)} %bitcast.12, bf16[448,1024]{1,0:T(8,128)(2,1)} %bitcast.14), custom_call_target="tpu_custom_call" | custom-call | tf_op jit(solution)/shard_map/update/pallas_call | solution.py:232
  (13 shorter events, 0.4 us)
Async XLA Ops:
  2.4 25.7 %all-to-all-start = ((bf16[16,32,512]{2,1,0:T(8,128)(2,1)}), bf16[16,32,512]{2,1,0:T(8,128)(2,1)S(1)}, u32[]{:S(2)}, u32[]{:S(2)}) async-start(bf16[16,32,512]{2,1,0:T(8,128)(2,1)} %broadcast_in_dim.2), calls=%async_computation | async-start | bytes 1048576 | tf_op jit(solution)/shard_map/all_to_all | solution.py:32
  13.4 5.1 %collective-permute-start = (bf16[32,1024]{1,0:T(8,128)(2,1)S(1)}, bf16[32,1024]{1,0:T(8,128)(2,1)S(1)}, u32[]{:S(2)}, u32[]{:S(2)}) collective-permute-start(bf16[32,1024]{1,0:T(8,128)(2,1)S(1)} %convert_element_type.11), channel_id=1, source_target_pairs={{0,128},{128,0},{1,129},{129,1},{2,130},{130,2},{3,131},{131,3},{4... | collective-permute-start | bytes 196616 | tf_op jit(solution)/shard_map/ppermute | solution.py:177
  18.5 4.2 %collective-permute-start.1 = (bf16[2,32,1024]{2,1,0:T(8,128)(2,1)S(1)}, bf16[2,32,1024]{2,1,0:T(8,128)(2,1)S(1)}, u32[]{:S(2)}, u32[]{:S(2)}) collective-permute-start(bf16[2,32,1024]{2,1,0:T(8,128)(2,1)S(1)} %pad_maximum_fusion.down0), channel_id=1, source_target_pairs={{0,32},{32,0},{64,96},{96,64},{1,33},{33,1},{65,97},{97,65},{2,34}... | collective-permute-start | bytes 393224 | tf_op jit(solution)/shard_map/ppermute | solution.py:178
  19.9 7.0 %collective-permute-start.2 = (bf16[2,32,1024]{2,1,0:T(8,128)(2,1)S(1)}, bf16[2,32,1024]{2,1,0:T(8,128)(2,1)S(1)}, u32[]{:S(2)}, u32[]{:S(2)}) collective-permute-start(bf16[2,32,1024]{2,1,0:T(8,128)(2,1)S(1)} %pad_maximum_fusion.down0), channel_id=1, source_target_pairs={{0,64},{32,96},{64,0},{96,32},{1,65},{33,97},{65,1},{97,33},{2,66}... | collective-permute-start | bytes 393224 | tf_op jit(solution)/shard_map/ppermute | solution.py:178
  22.5 5.6 %collective-permute-start.3 = (bf16[2,32,1024]{2,1,0:T(8,128)(2,1)S(1)}, bf16[2,32,1024]{2,1,0:T(8,128)(2,1)S(1)}, u32[]{:S(2)}, u32[]{:S(2)}) collective-permute-start(bf16[2,32,1024]{2,1,0:T(8,128)(2,1)S(1)} %pad_maximum_fusion.down0), channel_id=1, source_target_pairs={{0,96},{32,64},{64,32},{96,0},{1,97},{33,65},{65,33},{97,1},{2,98}... | collective-permute-start | bytes 393224 | tf_op jit(solution)/shard_map/ppermute | solution.py:178
  28.1 8.6 %collective-permute-start.4 = (bf16[16,32,512]{2,1,0:T(8,128)(2,1)S(1)}, bf16[16,32,512]{2,1,0:T(8,128)(2,1)S(1)}, u32[]{:S(2)}, u32[]{:S(2)}) collective-permute-start(bf16[16,32,512]{2,1,0:T(8,128)(2,1)S(1)} %all-to-all-done.ups), channel_id=1, source_target_pairs={{0,1},{1,0},{2,3},{3,2},{4,5},{5,4},{6,7},{7,6},{8,9},{9,8},{10,11... | collective-permute-start | bytes 1572872 | tf_op jit(solution)/shard_map/ppermute | solution.py:180
  31.3 0.9 copy-start
  32.2 0.8 copy-start.1
  36.6 6.1 %copy-start.3 = (f32[8,128]{1,0:T(8,128)}, f32[8,128]{1,0:T(8,128)S(1)}, u32[]{:S(2)}) copy-start(f32[8,128]{1,0:T(8,128)S(1)} %get-tuple-element.14.norms) | copy-start | bytes 12292
  36.7 6.0 %copy-start.2 = (s32[4]{0:T(128)}, s32[4]{0:T(128)S(1)}, u32[]{:S(2)}) copy-start(s32[4]{0:T(128)S(1)} %pad_add_fusion.place) | copy-start | bytes 52

commit v3 on v1

v3 whole, which is shorter than its diff:
```python
import jax
import jax.numpy as jnp
from jax import lax
from jax.experimental import pallas as pl
from jax.experimental.pallas import tpu as pltpu
from jax.sharding import Mesh, PartitionSpec as P

adapter_scale = 0.25
step_size = 0.1
norm_eps = 1e-06

GRP = ("xh", "y")
TP = ("xl", "z", "c")
PLANE = ("xh", "y", "xl")
COLUMN = ("z", "c")
f32, bf16 = jnp.float32, jnp.bfloat16
ALONG_LANES = (((1,), (1,)), ((), ()))
VMEM = pl.BlockSpec(memory_space=pltpu.VMEM)
SMEM = pl.BlockSpec(memory_space=pltpu.SMEM)
HBM = pl.BlockSpec(memory_space=pltpu.HBM)


def exchange(x, axes):
    return lax.all_to_all(x, axes, 0, 0, tiled=True)


def prepare_kernel(down_hbm, up_hbm, down, ups, factor_down, factor_up, sems):
    copies = [
        pltpu.make_async_copy(down_hbm, factor_down, sems.at[0]),
        pltpu.make_async_copy(up_hbm, factor_up, sems.at[1]),
    ]
    for copy in copies:
        copy.start()
    for copy in copies:
        copy.wait()
    down[...] = factor_down[...].astype(bf16)
    up = jnp.concatenate([factor_up[...], jnp.zeros((32, 64), f32)], 1)
    up = jnp.where(lax.axis_index("c") == 0, up, pltpu.roll(up, 64, 1)).astype(bf16)
    for k in range(16):
        ups[k] = up


def own_ranks_first(low, core):
    low = low.T
    return jnp.where(core == 0, low, jnp.concatenate([low[16:], low[:16]], 0)).astype(bf16)


def grad_b_kernel(
    place, tokens_hbm, grads_hbm, down0, down1, down2, down3, keep, give, tokens, grads, down, sems
):
    copies = []
    for n, (source, target) in enumerate(((tokens_hbm, tokens), (grads_hbm, grads))):
        width = source.shape[1] // 8
        for k in range(8):
            columns = pl.ds(width * k, width)
            copies.append(
                pltpu.make_async_copy(source.at[:, columns], target.at[:, columns], sems.at[8 * n + k])
            )
    for copy in copies:
        copy.start()
    for ky, blocks in enumerate((down0, down1, down2, down3)):
        for kx in range(2):
            owner = (place[0] ^ kx) * 4 + (place[1] ^ ky)
            down[:, pl.ds(pl.multiple_of(owner * 1024, 1024), 1024)] = blocks[kx]
    reduced = jnp.zeros((192, 32), f32)
    for q in range(4):
        columns = slice(2048 * q, 2048 * q + 2048)
        copies[2 * q].wait()
        copies[2 * q + 1].wait()
        reduced += lax.dot_general(
            tokens[:, columns], down[:, columns], ALONG_LANES, preferred_element_type=f32
        )
    left = own_ranks_first(reduced, place[3])
    for p in range(16):
        if p % 2 == 0:
            copies[8 + p // 2].wait()
        part = jnp.dot(left, grads[:, p * 896 : (p + 1) * 896], preferred_element_type=f32)
        keep[p] = part[:16].astype(bf16)
        give[p] = part[16:].astype(bf16)


def grad_a_kernel(place, tokens, grads, ups, ups_other, keep, give, up):
    for pair in range(16):
        mine, other = ups[pair], ups_other[pair]
        first = jnp.where(place[3] == 0, mine, other)
        second = jnp.where(place[3] == 0, other, mine)
        start = pair * 896
        up[:, start : start + 384] = first[:, :384]
        up[:, start + 384 : start + 512] = first[:, 384:] + second[:, :128]
        up[:, start + 512 : start + 896] = second[:, 128:]
    returned = lax.dot_general(grads[...], up[...], ALONG_LANES, preferred_element_type=f32)
    left = own_ranks_first(returned, place[3])
    for p in range(16):
        part = jnp.dot(left, tokens[:, p * 512 : (p + 1) * 512], preferred_element_type=f32)
        keep[p] = part[:16].astype(bf16)
        give[p] = part[16:].astype(bf16)


def chip_sum_kernel(keep_a, got_a, keep_b, got_b, out):
    for p in range(16):
        out[p, :, :512] = (keep_a[p].astype(f32) + got_a[p].astype(f32)).astype(bf16)
        out[p, :, 512:] = (keep_b[p].astype(f32) + got_b[p].astype(f32)).astype(bf16)


def plane_sum_kernel(parts, out, rows):
    for j in range(11):
        columns = slice(128 * j, 128 * j + 128)
        total = parts[0, :, columns].astype(f32)
        for k in range(1, 16):
            total += parts[k, :, columns].astype(f32)
        for i in range(2):
            rows[pl.ds(11 * i + j, 8, 23), :] = total[8 * i : 8 * i + 8]
    for z in range(8):
        out[z] = rows[pl.ds(23 * z, 22), :].astype(bf16)


def z_sum_kernel(parts, factor_down, factor_up, out, rows):
    total = parts[0].astype(f32)
    for k in range(1, 8):
        total += parts[k].astype(f32)
    total = adapter_scale * total
    squares = total * total

    def squared(*pieces):
        return sum(jnp.sum(squares[a:b], axis=0, keepdims=True) for a, b in pieces)

    down, up = factor_down[...], factor_up[...]
    rows[...] = jnp.zeros((32, 128), f32)
    rows[pl.ds(0, 22), :] = total
    sums = (
        squared((0, 4), (11, 15)),
        squared((4, 11), (15, 22)),
        jnp.full((1, 128), jnp.sum(down * down) * (1 / 4096), f32),
        jnp.full((1, 128), jnp.sum(up * up) * (1 / 1024), f32),
    )
    for k, line in enumerate(sums):
        high = line.astype(bf16).astype(f32)
        rows[pl.ds(24 + k, 1), :] = high
        rows[pl.ds(28 + k, 1), :] = line - high
    block = rows[...].astype(bf16)
    for k in range(16):
        out[k] = block


def reroute_kernel(place, parts, out, rows):
    group, half = place[0] * 4 + place[1], place[2]
    sums = jnp.zeros((4, 128), f32)
    for p in range(16):
        block = parts[p].astype(f32)
        sums += block[24:28] + block[28:32]
    high = sums.astype(bf16).astype(f32)
    low = sums - high
    mine = [parts[2 * group + k].astype(f32) for k in range(2)]
    for z in range(8):
        block = parts[8 * half + z].astype(f32)
        for core in range(2):
            k = 2 * z + core
            for i in range(2):
                rows[k, pl.ds(16 * i, 4), :] = mine[0][11 * i : 11 * i + 4]
                rows[k, pl.ds(16 * i + 4, 4), :] = mine[1][11 * i : 11 * i + 4]
                start = 11 * i + 4 + 3 * core
                rows[k, pl.ds(16 * i + 8, 4), :] = block[start : start + 4]
                rows[k, pl.ds(16 * i + 12, 4), :] = low if i else high
            out[k] = rows[k].astype(bf16)


def update_kernel(place, parts, factor_down, factor_up, base, new_down, new_up, merged, rows):
    sums = jnp.zeros((4, 128), f32)
    for k in range(16):
        block = parts[k].astype(f32)
        rows[pl.ds(k * 33, 32), :] = block
        sums += block[12:16] + block[28:32]
    sums = jnp.sum(sums, axis=1, keepdims=True)
    scale_a = step_size * jnp.sqrt(sums[2:3]) / jnp.sqrt(sums[0:1] + norm_eps)
    scale_b = step_size * jnp.sqrt(sums[3:4]) / jnp.sqrt(sums[1:2] + norm_eps)

    def ranks(j):
        tiles = [rows[pl.ds(33 * core + 16 * i + j, 8, 66), :] for core in range(2) for i in range(2)]
        return jnp.concatenate(tiles, 0)

    for j in range(8):
        columns = slice(128 * j, 128 * j + 128)
        new_down[:, columns] = factor_down[:, columns] - scale_a * ranks(j)
    grad_b = jnp.concatenate([ranks(8 + j) for j in range(4)], 1)
    grad_b = jnp.where(place[3] == 0, grad_b, pltpu.roll(grad_b, 448, 1))[:, :448]
    new_up[...] = factor_up[...] - scale_b * grad_b
    left = new_up[...].T.astype(bf16)
    right = new_down[...].astype(bf16)
    for k in range(7):
        lines = slice(64 * k, 64 * k + 64)
        product = jnp.dot(left[lines], right, preferred_element_type=f32)
        merged[lines] = (base[lines].astype(f32) + adapter_scale * product).astype(bf16)


def kernel(body, outs, args, scratch=(), in_hbm=(), mib=16, flops=0, moved=0):
    specs, placed = [], []
    for n, a in enumerate(args):
        if jnp.issubdtype(a.dtype, jnp.integer):
            specs.append(SMEM)
        else:
            specs.append(HBM if n in in_hbm else VMEM)
            a = pltpu.with_memory_space_constraint(a, pltpu.HBM if n in in_hbm else pltpu.VMEM)
        placed.append(a)
    return pl.pallas_call(
        body,
        out_shape=outs,
        in_specs=specs,
        out_specs=jax.tree.map(lambda _: VMEM, outs),
        scratch_shapes=list(scratch),
        compiler_params=pltpu.CompilerParams(vmem_limit_bytes=mib * 1024 * 1024),
        cost_estimate=pl.CostEstimate(flops=flops, bytes_accessed=moved, transcendentals=0),
        name=body.__name__,
    )(*placed)


def swap(x, axis):
    return lax.ppermute(x, axis, [(0, 1), (1, 0)])


def shards(tokens, grad_up, factor_down, factor_up, base_weight):
    place = jnp.stack([lax.axis_index(name) for name in ("xh", "y", "xl", "c")]).astype(jnp.int32)
    factor_up = factor_up.T
    shape = jax.ShapeDtypeStruct

    down, up = kernel(
        prepare_kernel,
        (shape((32, 1024), bf16), shape((16, 32, 512), bf16)),
        (factor_down, factor_up),
        [pltpu.VMEM((32, 1024), f32), pltpu.VMEM((32, 448), f32), pltpu.SemaphoreType.DMA((2,))],
        in_hbm=(0, 1),
    )
    down_far = swap(down, "xh")
    ups = exchange(up, ("xl", "z"))
    down0 = jnp.stack([down, down_far])
    downs = [down0] + [lax.ppermute(down0, "y", [(i, i ^ k) for i in range(4)]) for k in (1, 2, 3)]
    ups, downs = lax.optimization_barrier((ups, downs))
    ups_other = swap(ups, "c")

    keep_b, give_b, tokens, grad_up = kernel(
        grad_b_kernel,
        [shape((16, 16, 896), bf16)] * 2 + [pltpu.VMEM((192, 8192), bf16), pltpu.VMEM((192, 14336), bf16)],
        [place, tokens, grad_up] + downs,
        [pltpu.VMEM((32, 8192), bf16), pltpu.SemaphoreType.DMA((16,))],
        in_hbm=(1, 2),
        flops=300000000,
        moved=10 * 1024 * 1024,
    )
    got_b = swap(give_b, "c")
    keep_a, give_a = kernel(
        grad_a_kernel,
        [shape((16, 16, 512), bf16)] * 2,
        (place, tokens, grad_up, ups, ups_other),
        [pltpu.VMEM((32, 14336), bf16)],
        flops=300000000,
        moved=10 * 1024 * 1024,
    )
    got_a = swap(give_a, "c")
    args = (keep_a, got_a, keep_b, got_b)
    parts = kernel(chip_sum_kernel, shape((16, 16, 1408), bf16), args)
    parts = exchange(parts, PLANE)
    parts = kernel(plane_sum_kernel, shape((8, 22, 128), bf16), (parts,), [pltpu.VMEM((184, 128), f32)])
    parts = exchange(parts, "z")
    blocks = shape((16, 32, 128), bf16)
    parts = kernel(z_sum_kernel, blocks, (parts, factor_down, factor_up), [pltpu.VMEM((32, 128), f32)])
    parts = exchange(parts, PLANE)
    parts = kernel(reroute_kernel, blocks, (place, parts), [pltpu.VMEM((16, 32, 128), f32)])
    parts = exchange(parts, COLUMN)
    outs = (shape((32, 1024), f32), shape((32, 448), f32), shape((448, 1024), bf16))
    args = (place, parts, factor_down, factor_up, base_weight.T)
    new_down, new_up, merged = kernel(update_kernel, outs, args, [pltpu.VMEM((528, 128), f32)])
    return (new_down, new_up.T, merged.T)


def solution(mesh):
    fine = Mesh(mesh.devices.reshape(2, 4, 2, 8, 2), ("xh", "y", "xl", "z", "c"))
    return jax.shard_map(
        shards,
        mesh=fine,
        in_specs=(
            P(GRP + TP, None),
            P(GRP + TP, None),
            P(None, GRP),
            P(TP, None),
            P(GRP, TP),
        ),
        out_specs=(P(None, GRP), P(TP, None), P(GRP, TP)),
        check_vma=False,
    )
```

time: 142 us -> 103 us (0.73)
  matrix products: 16 us -> 0 us
  local copies, waits for them, and re-layouts: 15.6 us -> 0.02 us
  Pallas kernels: 0 us -> 14.9 us
  waiting for transfers between devices: 21.3 us -> 8.85 us
  blocking collectives: 45.6 us -> 58 us
  other arithmetic: 10.3 us -> 0.09 us
  starting transfers between devices: 27.2 us -> 20.1 us
  between operations: 4.94 us -> 0.71 us
    all_to_all x4 -> x1, waiting for transfers between devices: 21.3 us -> 0.62 us  [exchange(): return lax.all_to_all(x, axes, 0, 0, tiled=True)]
    all_to_all x2 -> x4, blocking collectives: 37.7 us -> 58 us  [exchange(): return lax.all_to_all(x, axes, 0, 0, tiled=True)]
    all_to_all x4 -> x1, starting transfers between devices: 27.2 us -> 10.1 us  [exchange(): return lax.all_to_all(x, axes, 0, 0, tiled=True)]
    dot_general x3 -> x0, matrix products: 16 us -> none  [the longest x1 6.83 us: shards(): lax.dot_general(reduced, grad_up, contract_first, preferred_element_type=...]
    pallas_call x0 -> x8, Pallas kernels: none -> 14.9 us  [kernel(): pl.pallas_call(body, out_shape=outs, in_specs=specs, out_specs=jax.tree.m...]
    ppermute x0 -> x7, starting transfers between devices: none -> 10.1 us  [the longest x4 6.56 us: swap(): return lax.ppermute(x, axis, [(0, 1), (1, 0)])]
    ppermute x0 -> x7, waiting for transfers between devices: none -> 8.23 us  [the longest x3 4.79 us: shards(): lax.ppermute(down0, 'y', [(i, i ^ k) for i in range(4)])]
    all_gather x2 -> x0, blocking collectives: 7.85 us -> none  [the longest x1 4.19 us: shards(): downs = lax.all_gather(downs, 'c', axis=0)]
  transfers between devices with their start and end apart: 4 -> 8, of which waited for: 3 -> 5; matrix products, arithmetic and copies ran while one was open for 9% -> 0% of each run, Pallas kernels for 0% -> 10%
where the time goes in v3:
time: 103 us
  blocking collectives  58 us (56%)
  starting transfers between devices  20.1 us (20%)
  Pallas kernels  14.9 us (14%)
  waiting for transfers between devices  8.85 us (9%)
    all_to_all x4, blocking collectives, exchange(): return lax.all_to_all(x, axes, 0, 0, tiled=True)  58 us
    pallas_call x8, Pallas kernels, kernel(): pl.pallas_call(body, out_shape=outs, in_specs=specs, out_specs=jax.tree.m...  14.9 us
    all_to_all x1, starting transfers between devices, exchange(): return lax.all_to_all(x, axes, 0, 0, tiled=True)  10.1 us
    ppermute x4, starting transfers between devices, swap(): return lax.ppermute(x, axis, [(0, 1), (1, 0)])  6.56 us
    ppermute x3, waiting for transfers between devices, shards(): lax.ppermute(down0, 'y', [(i, i ^ k) for i in range(4)])  4.79 us
    ppermute x3, starting transfers between devices, shards(): lax.ppermute(down0, 'y', [(i, i ^ k) for i in range(4)])  3.5 us
    ppermute x4, waiting for transfers between devices, swap(): return lax.ppermute(x, axis, [(0, 1), (1, 0)])  3.45 us
  transfers between devices with their start and end apart: 8, of which 5 were waited for; matrix products, arithmetic and copies ran while one was open for 0% of the time, Pallas kernels for 10%

profile of v3, /device:TPU:1, one launch (start us, length us, event | category | flops | bytes accessed | tf_op | source)
XLA Modules:
  0.0 102.8 jit_solution(2629527374017764787)
XLA Ops:
  0.6 1.8 %prepare_kernel.1 = (bf16[32,1024]{1,0:T(8,128)(2,1)S(1)}, bf16[16,32,512]{2,1,0:T(8,128)(2,1)}) custom-call(f32[32,1024]{1,0:T(8,128)} %factor_down.3, f32[32,448]{1,0:T(8,128)} %bitcast.11), custom_call_target="tpu_custom_call" | custom-call | tf_op jit(solution)/shard_map/prepare_kernel/pallas_call | solution.py:204
  2.5 10.1 %all-to-all-start = ((bf16[16,32,512]{2,1,0:T(8,128)(2,1)}), bf16[16,32,512]{2,1,0:T(8,128)(2,1)S(1)}, u32[]{:S(2)}, u32[]{:S(2)}) async-start(bf16[16,32,512]{2,1,0:T(8,128)(2,1)} %get-tuple-element.19), calls=%async_computation | async-start | bytes 1048576 | tf_op jit(solution)/shard_map/all_to_all | solution.py:24
  12.5 2.5 %collective-permute-start = (bf16[32,1024]{1,0:T(8,128)(2,1)S(1)}, bf16[32,1024]{1,0:T(8,128)(2,1)S(1)}, u32[]{:S(2)}, u32[]{:S(2)}) collective-permute-start(bf16[32,1024]{1,0:T(8,128)(2,1)S(1)} %get-tuple-element.20), channel_id=1, source_target_pairs={{0,128},{128,0},{1,129},{129,1},{2,130},{130,2},{3,131},{131,3},{4... | collective-permute-start | bytes 196616 | tf_op jit(solution)/shard_map/ppermute | solution.py:217
  15.1 2.3 %collective-permute-done = bf16[32,1024]{1,0:T(8,128)(2,1)S(1)} collective-permute-done((bf16[32,1024]{1,0:T(8,128)(2,1)S(1)}, bf16[32,1024]{1,0:T(8,128)(2,1)S(1)}, u32[]{:S(2)}, u32[]{:S(2)}) %collective-permute-start) | collective-permute-done | bytes 65568 | tf_op jit(solution)/shard_map/ppermute | solution.py:217
  17.4 2.8 %collective-permute-start.3 = (bf16[2,32,1024]{2,1,0:T(8,128)(2,1)S(1)}, bf16[2,32,1024]{2,1,0:T(8,128)(2,1)S(1)}, u32[]{:S(2)}, u32[]{:S(2)}) collective-permute-start(bf16[2,32,1024]{2,1,0:T(8,128)(2,1)S(1)} %pad_maximum_fusion.down0), channel_id=1, source_target_pairs={{0,96},{32,64},{64,32},{96,0},{1,97},{33,65},{65,33},{97,1},{2,98}... | collective-permute-start | bytes 393224 | tf_op jit(solution)/shard_map/ppermute | solution.py:235
  20.2 0.3 collective-permute-start.2
  20.6 0.3 collective-permute-start.1
  20.9 2.6 %collective-permute-done.3.down3 = bf16[2,32,1024]{2,1,0:T(8,128)(2,1)S(1)} collective-permute-done((bf16[2,32,1024]{2,1,0:T(8,128)(2,1)S(1)}, bf16[2,32,1024]{2,1,0:T(8,128)(2,1)S(1)}, u32[]{:S(2)}, u32[]{:S(2)}) %collective-permute-start.3) | collective-permute-done | bytes 131104 | tf_op jit(solution)/shard_map/ppermute | solution.py:235
  23.5 2.1 %collective-permute-done.2.down2 = bf16[2,32,1024]{2,1,0:T(8,128)(2,1)S(1)} collective-permute-done((bf16[2,32,1024]{2,1,0:T(8,128)(2,1)S(1)}, bf16[2,32,1024]{2,1,0:T(8,128)(2,1)S(1)}, u32[]{:S(2)}, u32[]{:S(2)}) %collective-permute-start.2) | collective-permute-done | bytes 131104 | tf_op jit(solution)/shard_map/ppermute | solution.py:235
  25.7 0.6 all-to-all-done.ups
  26.3 3.4 %collective-permute-start.4 = (bf16[16,32,512]{2,1,0:T(8,128)(2,1)S(1)}, bf16[16,32,512]{2,1,0:T(8,128)(2,1)S(1)}, u32[]{:S(2)}, u32[]{:S(2)}) collective-permute-start(bf16[16,32,512]{2,1,0:T(8,128)(2,1)S(1)} %all-to-all-done.ups), channel_id=1, source_target_pairs={{0,1},{1,0},{2,3},{3,2},{4,5},{5,4},{6,7},{7,6},{8,9},{9,8},{10,11... | collective-permute-start | bytes 1572872 | tf_op jit(solution)/shard_map/ppermute | solution.py:217
  29.7 6.5 %grad_b_kernel.1 = (bf16[16,16,896]{2,1,0:T(8,128)(2,1)S(1)}, bf16[16,16,896]{2,1,0:T(8,128)(2,1)S(1)}, bf16[192,8192]{1,0:T(8,128)(2,1)S(1)}, bf16[192,14336]{1,0:T(8,128)(2,1)S(1)}) custom-call(s32[4]{0:T(128)S(1)} %pad_add_fusion.place, bf16[192,8192]{1,0:T(8,128)(2,1)} %tokens_hbm.1, bf16[192,14336]{1,0:T(8,128)(2,1)} %grads_hbm.1, ...), custom_call_target="tpu_custom_call" | custom-call | flops 300000000 | bytes 10485760 | tf_op jit(solution)/shard_map/grad_b_kernel/pallas_call | solution.py:204
  36.4 3.5 %grad_a_kernel.1 = (bf16[16,16,512]{2,1,0:T(8,128)(2,1)S(1)}, bf16[16,16,512]{2,1,0:T(8,128)(2,1)S(1)}) custom-call(s32[4]{0:T(128)S(1)} %pad_add_fusion.place, bf16[192,8192]{1,0:T(8,128)(2,1)S(1)} %get-tuple-element.25.tokens, bf16[192,14336]{1,0:T(8,128)(2,1)S(1)} %get-tuple-element.26.grads, bf16[16,32,512]{2,1,0:T(8,128)(2,1)S(1)} %all-to-all-done.ups, ...), custom_call_target="tpu_custom_call" | custom-call | flops 300000000 | bytes 10485760 | tf_op jit(solution)/shard_map/grad_a_kernel/pallas_call | solution.py:204
  39.9 0.6 collective-permute-start.5
  40.4 1.2 %collective-permute-done.5.got_a = bf16[16,16,512]{2,1,0:T(8,128)(2,1)S(1)} collective-permute-done((bf16[16,16,512]{2,1,0:T(8,128)(2,1)S(1)}, bf16[16,16,512]{2,1,0:T(8,128)(2,1)S(1)}, u32[]{:S(2)}, u32[]{:S(2)}) %collective-permute-start.5) | collective-permute-done | bytes 262176 | tf_op jit(solution)/shard_map/ppermute | solution.py:217
  41.6 0.2 chip_sum_kernel.1
  41.8 18.9 %all_to_all.25.parts = bf16[16,16,1408]{2,1,0:T(8,128)(2,1)S(1)} all-to-all(bf16[16,16,1408]{2,1,0:T(8,128)(2,1)S(1)} %chip_sum_kernel.1), channel_id=1, replica_groups=mesh['xh'=2,'y'=4,'xl'=2,'z'=8,'c'=2] {'xh','y','xl'}, dimensions={0} | all-to-all | bytes 1441792 | tf_op jit(solution)/shard_map/all_to_all | solution.py:24
  60.7 0.1 plane_sum_kernel.1
  60.8 13.7 %all_to_all.26.parts = bf16[8,22,128]{2,1,0:T(8,128)(2,1)S(1)} all-to-all(bf16[8,22,128]{2,1,0:T(8,128)(2,1)S(1)} %plane_sum_kernel.1), channel_id=1, replica_groups=mesh['xh'=2,'y'=4,'xl'=2,'z'=8,'c'=2] {'z'}, dimensions={0} | all-to-all | bytes 90112 | tf_op jit(solution)/shard_map/all_to_all | solution.py:24
  74.5 0.2 z_sum_kernel.1
  74.7 10.0 %all_to_all.27.parts = bf16[16,32,128]{2,1,0:T(8,128)(2,1)S(1)} all-to-all(bf16[16,32,128]{2,1,0:T(8,128)(2,1)S(1)} %z_sum_kernel.1), channel_id=1, replica_groups=mesh['xh'=2,'y'=4,'xl'=2,'z'=8,'c'=2] {'xh','y','xl'}, dimensions={0} | all-to-all | bytes 262144 | tf_op jit(solution)/shard_map/all_to_all | solution.py:24
  84.7 0.6 reroute_kernel.1
  85.3 15.4 %all_to_all.28.parts = bf16[16,32,128]{2,1,0:T(8,128)(2,1)S(1)} all-to-all(bf16[16,32,128]{2,1,0:T(8,128)(2,1)S(1)} %reroute_kernel.1), channel_id=1, replica_groups=mesh['xh'=2,'y'=4,'xl'=2,'z'=8,'c'=2] {'z','c'}, dimensions={0} | all-to-all | bytes 262144 | tf_op jit(solution)/shard_map/all_to_all | solution.py:24
  100.7 2.1 %update_kernel.1 = (f32[32,1024]{1,0:T(8,128)}, f32[32,448]{1,0:T(8,128)}, bf16[448,1024]{1,0:T(8,128)(2,1)}) custom-call(s32[4]{0:T(128)S(1)} %pad_add_fusion.place, bf16[16,32,128]{2,1,0:T(8,128)(2,1)S(1)} %all_to_all.28.parts, f32[32,1024]{1,0:T(8,128)S(1)} %copy-done, f32[32,448]{1,0:T(8,128)S(1)} %bitcast.13, bf16[448,1024]{1,0:T(8,128)(2,1)S(1)} %bitcast.10), custom_call_target="tpu_custom_call" | custom-call | tf_op jit(solution)/shard_map/update_kernel/pallas_call | solution.py:204
  (12 shorter events, 0.2 us)
Async XLA Ops:
  2.5 23.8 %all-to-all-start = ((bf16[16,32,512]{2,1,0:T(8,128)(2,1)}), bf16[16,32,512]{2,1,0:T(8,128)(2,1)S(1)}, u32[]{:S(2)}, u32[]{:S(2)}) async-start(bf16[16,32,512]{2,1,0:T(8,128)(2,1)} %get-tuple-element.19), calls=%async_computation | async-start | bytes 1048576 | tf_op jit(solution)/shard_map/all_to_all | solution.py:24
  12.5 4.8 %collective-permute-start = (bf16[32,1024]{1,0:T(8,128)(2,1)S(1)}, bf16[32,1024]{1,0:T(8,128)(2,1)S(1)}, u32[]{:S(2)}, u32[]{:S(2)}) collective-permute-start(bf16[32,1024]{1,0:T(8,128)(2,1)S(1)} %get-tuple-element.20), channel_id=1, source_target_pairs={{0,128},{128,0},{1,129},{129,1},{2,130},{130,2},{3,131},{131,3},{4... | collective-permute-start | bytes 196616 | tf_op jit(solution)/shard_map/ppermute | solution.py:217
  17.4 6.1 %collective-permute-start.3 = (bf16[2,32,1024]{2,1,0:T(8,128)(2,1)S(1)}, bf16[2,32,1024]{2,1,0:T(8,128)(2,1)S(1)}, u32[]{:S(2)}, u32[]{:S(2)}) collective-permute-start(bf16[2,32,1024]{2,1,0:T(8,128)(2,1)S(1)} %pad_maximum_fusion.down0), channel_id=1, source_target_pairs={{0,96},{32,64},{64,32},{96,0},{1,97},{33,65},{65,33},{97,1},{2,98}... | collective-permute-start | bytes 393224 | tf_op jit(solution)/shard_map/ppermute | solution.py:235
  20.2 5.5 %collective-permute-start.2 = (bf16[2,32,1024]{2,1,0:T(8,128)(2,1)S(1)}, bf16[2,32,1024]{2,1,0:T(8,128)(2,1)S(1)}, u32[]{:S(2)}, u32[]{:S(2)}) collective-permute-start(bf16[2,32,1024]{2,1,0:T(8,128)(2,1)S(1)} %pad_maximum_fusion.down0), channel_id=1, source_target_pairs={{0,64},{32,96},{64,0},{96,32},{1,65},{33,97},{65,1},{97,33},{2,66}... | collective-permute-start | bytes 393224 | tf_op jit(solution)/shard_map/ppermute | solution.py:235
  20.6 5.1 %collective-permute-start.1 = (bf16[2,32,1024]{2,1,0:T(8,128)(2,1)S(1)}, bf16[2,32,1024]{2,1,0:T(8,128)(2,1)S(1)}, u32[]{:S(2)}, u32[]{:S(2)}) collective-permute-start(bf16[2,32,1024]{2,1,0:T(8,128)(2,1)S(1)} %pad_maximum_fusion.down0), channel_id=1, source_target_pairs={{0,32},{32,0},{64,96},{96,64},{1,33},{33,1},{65,97},{97,65},{2,34}... | collective-permute-start | bytes 393224 | tf_op jit(solution)/shard_map/ppermute | solution.py:235
  26.3 10.0 %collective-permute-start.4 = (bf16[16,32,512]{2,1,0:T(8,128)(2,1)S(1)}, bf16[16,32,512]{2,1,0:T(8,128)(2,1)S(1)}, u32[]{:S(2)}, u32[]{:S(2)}) collective-permute-start(bf16[16,32,512]{2,1,0:T(8,128)(2,1)S(1)} %all-to-all-done.ups), channel_id=1, source_target_pairs={{0,1},{1,0},{2,3},{3,2},{4,5},{5,4},{6,7},{7,6},{8,9},{9,8},{10,11... | collective-permute-start | bytes 1572872 | tf_op jit(solution)/shard_map/ppermute | solution.py:217
  36.2 4.2 %collective-permute-start.6 = (bf16[16,16,896]{2,1,0:T(8,128)(2,1)S(1)}, bf16[16,16,896]{2,1,0:T(8,128)(2,1)S(1)}, u32[]{:S(2)}, u32[]{:S(2)}) collective-permute-start(bf16[16,16,896]{2,1,0:T(8,128)(2,1)S(1)} %get-tuple-element.31), channel_id=1, source_target_pairs={{0,1},{1,0},{2,3},{3,2},{4,5},{5,4},{6,7},{7,6},{8,9},{9,8},{10,11... | collective-permute-start | bytes 1376264 | tf_op jit(solution)/shard_map/ppermute | solution.py:217
  36.3 38.2 %copy-start = (f32[32,1024]{1,0:T(8,128)S(1)}, f32[32,1024]{1,0:T(8,128)}, u32[]{:S(2)}) copy-start(f32[32,1024]{1,0:T(8,128)} %factor_down.3) | copy-start | bytes 393220
  36.3 38.2 %copy-start.2 = (f32[448,32]{0,1:T(8,128)S(1)}, f32[448,32]{0,1:T(8,128)}, u32[]{:S(2)}) copy-start(f32[448,32]{0,1:T(8,128)} %param.8) | copy-start | bytes 172036
  36.3 64.3 %copy-start.1 = (bf16[1024,448]{0,1:T(8,128)(2,1)S(1)}, bf16[1024,448]{0,1:T(8,128)(2,1)}, u32[]{:S(2)}) copy-start(bf16[1024,448]{0,1:T(8,128)(2,1)} %param.9) | copy-start | bytes 2752516
  39.9 1.7 %collective-permute-start.5 = (bf16[16,16,512]{2,1,0:T(8,128)(2,1)S(1)}, bf16[16,16,512]{2,1,0:T(8,128)(2,1)S(1)}, u32[]{:S(2)}, u32[]{:S(2)}) collective-permute-start(bf16[16,16,512]{2,1,0:T(8,128)(2,1)S(1)} %get-tuple-element.29), channel_id=1, source_target_pairs={{0,1},{1,0},{2,3},{3,2},{4,5},{5,4},{6,7},{7,6},{8,9},{9,8},{10,11... | collective-permute-start | bytes 786440 | tf_op jit(solution)/shard_map/ppermute | solution.py:217

commit v4 on v3

--- a/solution.py
+++ b/solution.py
@@ -12,7 +12,6 @@
 GRP = ("xh", "y")
 TP = ("xl", "z", "c")
 PLANE = ("xh", "y", "xl")
-COLUMN = ("z", "c")
 f32, bf16 = jnp.float32, jnp.bfloat16
 ALONG_LANES = (((1,), (1,)), ((), ()))
 VMEM = pl.BlockSpec(memory_space=pltpu.VMEM)
@@ -75,8 +74,8 @@
         if p % 2 == 0:
             copies[8 + p // 2].wait()
         part = jnp.dot(left, grads[:, p * 896 : (p + 1) * 896], preferred_element_type=f32)
-        keep[p] = part[:16].astype(bf16)
-        give[p] = part[16:].astype(bf16)
+        keep[:, p * 896 : (p + 1) * 896] = part[:16].astype(bf16)
+        give[:, p * 896 : (p + 1) * 896] = part[16:].astype(bf16)
 
 
 def grad_a_kernel(place, tokens, grads, ups, ups_other, keep, give, up):
@@ -92,90 +91,78 @@
     left = own_ranks_first(returned, place[3])
     for p in range(16):
         part = jnp.dot(left, tokens[:, p * 512 : (p + 1) * 512], preferred_element_type=f32)
-        keep[p] = part[:16].astype(bf16)
-        give[p] = part[16:].astype(bf16)
-
-
-def chip_sum_kernel(keep_a, got_a, keep_b, got_b, out):
-    for p in range(16):
-        out[p, :, :512] = (keep_a[p].astype(f32) + got_a[p].astype(f32)).astype(bf16)
-        out[p, :, 512:] = (keep_b[p].astype(f32) + got_b[p].astype(f32)).astype(bf16)
-
-
-def plane_sum_kernel(parts, out, rows):
-    for j in range(11):
-        columns = slice(128 * j, 128 * j + 128)
-        total = parts[0, :, columns].astype(f32)
-        for k in range(1, 16):
-            total += parts[k, :, columns].astype(f32)
-        for i in range(2):
-            rows[pl.ds(11 * i + j, 8, 23), :] = total[8 * i : 8 * i + 8]
-    for z in range(8):
-        out[z] = rows[pl.ds(23 * z, 22), :].astype(bf16)
-
-
-def z_sum_kernel(parts, factor_down, factor_up, out, rows):
+        keep[:, p * 512 : (p + 1) * 512] = part[:16].astype(bf16)
+        give[:, p * 512 : (p + 1) * 512] = part[16:].astype(bf16)
+
+
+def chip_sum_kernel(keep_a, got_a, keep_b, got_b, out, rows):
+    tile = 0
+    for keep, got in ((keep_a, got_a), (keep_b, got_b)):
+        for j in range(keep.shape[1] // 128):
+            columns = slice(128 * j, 128 * j + 128)
+            total = keep[:, columns].astype(f32) + got[:, columns].astype(f32)
+            for h in range(2):
+                rows[pl.ds(177 * 8 * h + tile, 8, 177), :] = total[8 * h : 8 * h + 8]
+            tile += 1
+    for r in range(16):
+        out[r] = rows[pl.ds(177 * r, 176), :].astype(bf16)
+
+
+def plane_sum_kernel(parts, factor_up, out, extra):
+    total = parts[0].astype(f32)
+    for k in range(1, 16):
+        total += parts[k].astype(f32)
+    up = factor_up[...]
+    line = jnp.full((1, 128), jnp.sum(up * up) * (1 / 8), f32)
+    high = line.astype(bf16).astype(f32)
+    extra[...] = jnp.zeros((16, 128), f32)
+    extra[0:1] = high
+    extra[1:2] = line - high
+    block, last = total.astype(bf16), extra[...].astype(bf16)
+    for k in range(8):
+        out[k, :176] = block
+        out[k, 176:] = last
+
+
+def reroute_kernel(parts, factor_down, out, row, rows):
     total = parts[0].astype(f32)
     for k in range(1, 8):
         total += parts[k].astype(f32)
-    total = adapter_scale * total
-    squares = total * total
-
-    def squared(*pieces):
-        return sum(jnp.sum(squares[a:b], axis=0, keepdims=True) for a, b in pieces)
-
-    down, up = factor_down[...], factor_up[...]
-    rows[...] = jnp.zeros((32, 128), f32)
-    rows[pl.ds(0, 22), :] = total
-    sums = (
-        squared((0, 4), (11, 15)),
-        squared((4, 11), (15, 22)),
-        jnp.full((1, 128), jnp.sum(down * down) * (1 / 4096), f32),
-        jnp.full((1, 128), jnp.sum(up * up) * (1 / 1024), f32),
-    )
-    for k, line in enumerate(sums):
-        high = line.astype(bf16).astype(f32)
-        rows[pl.ds(24 + k, 1), :] = high
-        rows[pl.ds(28 + k, 1), :] = line - high
-    block = rows[...].astype(bf16)
-    for k in range(16):
-        out[k] = block
-
-
-def reroute_kernel(place, parts, out, rows):
-    group, half = place[0] * 4 + place[1], place[2]
-    sums = jnp.zeros((4, 128), f32)
+    grads = adapter_scale * total[:176]
+    row[...] = grads
+    squares = grads * grads
+    down = factor_down[...]
+    lane = lax.broadcasted_iota(jnp.int32, (1, 128), 1)
+    line = jnp.where(
+        lane < 64,
+        jnp.where(lane < 32, jnp.sum(squares[:64]), jnp.sum(squares[64:])),
+        jnp.where(lane < 96, jnp.sum(down * down) * (1 / 4), total[176:177] + total[177:178]),
+    )
+    high = line.astype(bf16).astype(f32)
+    low = line - high
+    z = lax.axis_index("z")
     for p in range(16):
-        block = parts[p].astype(f32)
-        sums += block[24:28] + block[28:32]
-    high = sums.astype(bf16).astype(f32)
-    low = sums - high
-    mine = [parts[2 * group + k].astype(f32) for k in range(2)]
-    for z in range(8):
-        block = parts[8 * half + z].astype(f32)
         for core in range(2):
-            k = 2 * z + core
-            for i in range(2):
-                rows[k, pl.ds(16 * i, 4), :] = mine[0][11 * i : 11 * i + 4]
-                rows[k, pl.ds(16 * i + 4, 4), :] = mine[1][11 * i : 11 * i + 4]
-                start = 11 * i + 4 + 3 * core
-                rows[k, pl.ds(16 * i + 8, 4), :] = block[start : start + 4]
-                rows[k, pl.ds(16 * i + 12, 4), :] = low if i else high
+            k = 2 * p + core
+            rows[k, 0:8] = row[8 * (p // 2) : 8 * (p // 2) + 8]
+            rows[k, 8:12] = row[pl.ds(64 + 7 * (8 * (p % 2) + z) + 3 * core, 4), :]
+            rows[k, 12:13] = high
+            rows[k, 13:14] = low
+            rows[k, 14:16] = jnp.zeros((2, 128), f32)
             out[k] = rows[k].astype(bf16)
 
 
 def update_kernel(place, parts, factor_down, factor_up, base, new_down, new_up, merged, rows):
-    sums = jnp.zeros((4, 128), f32)
-    for k in range(16):
+    line = jnp.zeros((1, 128), f32)
+    for k in range(32):
         block = parts[k].astype(f32)
-        rows[pl.ds(k * 33, 32), :] = block
-        sums += block[12:16] + block[28:32]
-    sums = jnp.sum(sums, axis=1, keepdims=True)
-    scale_a = step_size * jnp.sqrt(sums[2:3]) / jnp.sqrt(sums[0:1] + norm_eps)
-    scale_b = step_size * jnp.sqrt(sums[3:4]) / jnp.sqrt(sums[1:2] + norm_eps)
+        rows[pl.ds(k * 17, 16), :] = block
+        line += block[12:13] + block[13:14]
+    scale_a = step_size * jnp.sqrt(line[:, 64:65]) / jnp.sqrt(line[:, 0:1] + norm_eps)
+    scale_b = step_size * jnp.sqrt(line[:, 96:97]) / jnp.sqrt(line[:, 32:33] + norm_eps)
 
     def ranks(j):
-        tiles = [rows[pl.ds(33 * core + 16 * i + j, 8, 66), :] for core in range(2) for i in range(2)]
+        tiles = [rows[pl.ds(17 * core + 272 * h + j, 8, 34), :] for core in range(2) for h in range(2)]
         return jnp.concatenate(tiles, 0)
 
     for j in range(8):
@@ -238,7 +225,7 @@
 
     keep_b, give_b, tokens, grad_up = kernel(
         grad_b_kernel,
-        [shape((16, 16, 896), bf16)] * 2 + [pltpu.VMEM((192, 8192), bf16), pltpu.VMEM((192, 14336), bf16)],
+        [shape((16, 14336), bf16)] * 2 + [pltpu.VMEM((192, 8192), bf16), pltpu.VMEM((192, 14336), bf16)],
         [place, tokens, grad_up] + downs,
         [pltpu.VMEM((32, 8192), bf16), pltpu.SemaphoreType.DMA((16,))],
         in_hbm=(1, 2),
@@ -248,7 +235,7 @@
     got_b = swap(give_b, "c")
     keep_a, give_a = kernel(
         grad_a_kernel,
-        [shape((16, 16, 512), bf16)] * 2,
+        [shape((16, 8192), bf16)] * 2,
         (place, tokens, grad_up, ups, ups_other),
         [pltpu.VMEM((32, 14336), bf16)],
         flops=300000000,
@@ -256,18 +243,18 @@
     )
     got_a = swap(give_a, "c")
     args = (keep_a, got_a, keep_b, got_b)
-    parts = kernel(chip_sum_kernel, shape((16, 16, 1408), bf16), args)
+    parts = kernel(chip_sum_kernel, shape((16, 176, 128), bf16), args, [pltpu.VMEM((2832, 128), f32)])
     parts = exchange(parts, PLANE)
-    parts = kernel(plane_sum_kernel, shape((8, 22, 128), bf16), (parts,), [pltpu.VMEM((184, 128), f32)])
+    parts = kernel(
+        plane_sum_kernel, shape((8, 192, 128), bf16), (parts, factor_up), [pltpu.VMEM((16, 128), f32)]
+    )
     parts = exchange(parts, "z")
-    blocks = shape((16, 32, 128), bf16)
-    parts = kernel(z_sum_kernel, blocks, (parts, factor_down, factor_up), [pltpu.VMEM((32, 128), f32)])
-    parts = exchange(parts, PLANE)
-    parts = kernel(reroute_kernel, blocks, (place, parts), [pltpu.VMEM((16, 32, 128), f32)])
-    parts = exchange(parts, COLUMN)
+    scratch = [pltpu.VMEM((176, 128), f32), pltpu.VMEM((32, 16, 128), f32)]
+    parts = kernel(reroute_kernel, shape((32, 16, 128), bf16), (parts, factor_down), scratch)
+    parts = exchange(parts, PLANE + ("c",))
     outs = (shape((32, 1024), f32), shape((32, 448), f32), shape((448, 1024), bf16))
     args = (place, parts, factor_down, factor_up, base_weight.T)
-    new_down, new_up, merged = kernel(update_kernel, outs, args, [pltpu.VMEM((528, 128), f32)])
+    new_down, new_up, merged = kernel(update_kernel, outs, args, [pltpu.VMEM((544, 128), f32)])
     return (new_down, new_up.T, merged.T)
 
 

time: 103 us -> 97 us (0.942)
  blocking collectives: 58 us -> 52.3 us
    all_to_all x4 -> x3, blocking collectives: 58 us -> 52.3 us  [exchange(): return lax.all_to_all(x, axes, 0, 0, tiled=True)]
    pallas_call x8 -> x7, Pallas kernels: 14.9 us -> 14.6 us  [kernel(): pl.pallas_call(body, out_shape=outs, in_specs=specs, out_specs=jax.tree.m...]
where the time goes in v4:
time: 97 us; the launch traced here: 96.7 us
  blocking collectives  52.3 us (54%)
  starting transfers between devices  20.1 us (21%)
  Pallas kernels  14.6 us (15%)
  waiting for transfers between devices  8.85 us (9%)
    all_to_all x3, blocking collectives, exchange(): return lax.all_to_all(x, axes, 0, 0, tiled=True)  52.3 us
    pallas_call x7, Pallas kernels, kernel(): pl.pallas_call(body, out_shape=outs, in_specs=specs, out_specs=jax.tree.m...  14.6 us
    all_to_all x1, starting transfers between devices, exchange(): return lax.all_to_all(x, axes, 0, 0, tiled=True)  10.1 us
    ppermute x4, starting transfers between devices, swap(): return lax.ppermute(x, axis, [(0, 1), (1, 0)])  6.56 us
    ppermute x3, waiting for transfers between devices, shards(): lax.ppermute(down0, 'y', [(i, i ^ k) for i in range(4)])  4.79 us
    ppermute x3, starting transfers between devices, shards(): lax.ppermute(down0, 'y', [(i, i ^ k) for i in range(4)])  3.5 us
    ppermute x4, waiting for transfers between devices, swap(): return lax.ppermute(x, axis, [(0, 1), (1, 0)])  3.45 us
  transfers between devices with their start and end apart: 8, of which 5 were waited for; matrix products, arithmetic and copies ran while one was open for 0% of the time, Pallas kernels for 10%

profile of v4, /device:TPU:1, one launch (start us, length us, event | category | flops | bytes accessed | tf_op | source)
XLA Modules:
  0.0 96.7 jit_solution(588368097712534293)
XLA Ops:
  0.6 1.8 %prepare_kernel.1 = (bf16[32,1024]{1,0:T(8,128)(2,1)S(1)}, bf16[16,32,512]{2,1,0:T(8,128)(2,1)}) custom-call(f32[32,1024]{1,0:T(8,128)} %factor_down.3, f32[32,448]{1,0:T(8,128)} %bitcast.11), custom_call_target="tpu_custom_call" | custom-call | tf_op jit(solution)/shard_map/prepare_kernel/pallas_call | solution.py:191
  2.5 10.1 %all-to-all-start = ((bf16[16,32,512]{2,1,0:T(8,128)(2,1)}), bf16[16,32,512]{2,1,0:T(8,128)(2,1)S(1)}, u32[]{:S(2)}, u32[]{:S(2)}) async-start(bf16[16,32,512]{2,1,0:T(8,128)(2,1)} %get-tuple-element.19), calls=%async_computation | async-start | bytes 1048576 | tf_op jit(solution)/shard_map/all_to_all | solution.py:23
  12.5 2.5 %collective-permute-start = (bf16[32,1024]{1,0:T(8,128)(2,1)S(1)}, bf16[32,1024]{1,0:T(8,128)(2,1)S(1)}, u32[]{:S(2)}, u32[]{:S(2)}) collective-permute-start(bf16[32,1024]{1,0:T(8,128)(2,1)S(1)} %get-tuple-element.20), channel_id=1, source_target_pairs={{0,128},{128,0},{1,129},{129,1},{2,130},{130,2},{3,131},{131,3},{4... | collective-permute-start | bytes 196616 | tf_op jit(solution)/shard_map/ppermute | solution.py:204
  15.1 2.3 %collective-permute-done = bf16[32,1024]{1,0:T(8,128)(2,1)S(1)} collective-permute-done((bf16[32,1024]{1,0:T(8,128)(2,1)S(1)}, bf16[32,1024]{1,0:T(8,128)(2,1)S(1)}, u32[]{:S(2)}, u32[]{:S(2)}) %collective-permute-start) | collective-permute-done | bytes 65568 | tf_op jit(solution)/shard_map/ppermute | solution.py:204
  17.4 2.8 %collective-permute-start.3 = (bf16[2,32,1024]{2,1,0:T(8,128)(2,1)S(1)}, bf16[2,32,1024]{2,1,0:T(8,128)(2,1)S(1)}, u32[]{:S(2)}, u32[]{:S(2)}) collective-permute-start(bf16[2,32,1024]{2,1,0:T(8,128)(2,1)S(1)} %pad_maximum_fusion.down0), channel_id=1, source_target_pairs={{0,96},{32,64},{64,32},{96,0},{1,97},{33,65},{65,33},{97,1},{2,98}... | collective-permute-start | bytes 393224 | tf_op jit(solution)/shard_map/ppermute | solution.py:222
  20.2 0.3 collective-permute-start.2
  20.6 0.3 collective-permute-start.1
  20.9 2.6 %collective-permute-done.3.down3 = bf16[2,32,1024]{2,1,0:T(8,128)(2,1)S(1)} collective-permute-done((bf16[2,32,1024]{2,1,0:T(8,128)(2,1)S(1)}, bf16[2,32,1024]{2,1,0:T(8,128)(2,1)S(1)}, u32[]{:S(2)}, u32[]{:S(2)}) %collective-permute-start.3) | collective-permute-done | bytes 131104 | tf_op jit(solution)/shard_map/ppermute | solution.py:222
  23.5 2.1 %collective-permute-done.2.down2 = bf16[2,32,1024]{2,1,0:T(8,128)(2,1)S(1)} collective-permute-done((bf16[2,32,1024]{2,1,0:T(8,128)(2,1)S(1)}, bf16[2,32,1024]{2,1,0:T(8,128)(2,1)S(1)}, u32[]{:S(2)}, u32[]{:S(2)}) %collective-permute-start.2) | collective-permute-done | bytes 131104 | tf_op jit(solution)/shard_map/ppermute | solution.py:222
  25.7 0.6 all-to-all-done.ups
  26.3 3.4 %collective-permute-start.4 = (bf16[16,32,512]{2,1,0:T(8,128)(2,1)S(1)}, bf16[16,32,512]{2,1,0:T(8,128)(2,1)S(1)}, u32[]{:S(2)}, u32[]{:S(2)}) collective-permute-start(bf16[16,32,512]{2,1,0:T(8,128)(2,1)S(1)} %all-to-all-done.ups), channel_id=1, source_target_pairs={{0,1},{1,0},{2,3},{3,2},{4,5},{5,4},{6,7},{7,6},{8,9},{9,8},{10,11... | collective-permute-start | bytes 1572872 | tf_op jit(solution)/shard_map/ppermute | solution.py:204
  29.7 0.1 pad_add_fusion.place
  29.7 6.5 %grad_b_kernel.1 = (bf16[16,14336]{1,0:T(8,128)(2,1)S(1)}, bf16[16,14336]{1,0:T(8,128)(2,1)S(1)}, bf16[192,8192]{1,0:T(8,128)(2,1)S(1)}, bf16[192,14336]{1,0:T(8,128)(2,1)S(1)}) custom-call(s32[4]{0:T(128)S(1)} %pad_add_fusion.place, bf16[192,8192]{1,0:T(8,128)(2,1)} %tokens_hbm.1, bf16[192,14336]{1,0:T(8,128)(2,1)} %grads_hbm.1, ...), custom_call_target="tpu_custom_call" | custom-call | flops 300000000 | bytes 10485760 | tf_op jit(solution)/shard_map/grad_b_kernel/pallas_call | solution.py:191
  36.2 0.1 collective-permute-start.6
  36.3 3.5 %grad_a_kernel.1 = (bf16[16,8192]{1,0:T(8,128)(2,1)S(1)}, bf16[16,8192]{1,0:T(8,128)(2,1)S(1)}) custom-call(s32[4]{0:T(128)S(1)} %pad_add_fusion.place, bf16[192,8192]{1,0:T(8,128)(2,1)S(1)} %get-tuple-element.25.tokens, bf16[192,14336]{1,0:T(8,128)(2,1)S(1)} %get-tuple-element.26.grads, bf16[16,32,512]{2,1,0:T(8,128)(2,1)S(1)} %all-to-all-done.ups, ...), custom_call_target="tpu_custom_call" | custom-call | flops 300000000 | bytes 10485760 | tf_op jit(solution)/shard_map/grad_a_kernel/pallas_call | solution.py:191
  39.9 0.6 collective-permute-start.5
  40.4 1.2 %collective-permute-done.5.got_a = bf16[16,8192]{1,0:T(8,128)(2,1)S(1)} collective-permute-done((bf16[16,8192]{1,0:T(8,128)(2,1)S(1)}, bf16[16,8192]{1,0:T(8,128)(2,1)S(1)}, u32[]{:S(2)}, u32[]{:S(2)}) %collective-permute-start.5) | collective-permute-done | bytes 262176 | tf_op jit(solution)/shard_map/ppermute | solution.py:204
  41.6 0.2 chip_sum_kernel.1
  41.8 18.9 %all_to_all.20.parts = bf16[16,176,128]{2,1,0:T(8,128)(2,1)S(1)} all-to-all(bf16[16,176,128]{2,1,0:T(8,128)(2,1)S(1)} %chip_sum_kernel.1), channel_id=1, replica_groups=mesh['xh'=2,'y'=4,'xl'=2,'z'=8,'c'=2] {'xh','y','xl'}, dimensions={0} | all-to-all | bytes 1441792 | tf_op jit(solution)/shard_map/all_to_all | solution.py:23
  60.7 0.2 plane_sum_kernel.1
  60.9 19.0 %all_to_all.21.parts = bf16[8,192,128]{2,1,0:T(8,128)(2,1)S(1)} all-to-all(bf16[8,192,128]{2,1,0:T(8,128)(2,1)S(1)} %plane_sum_kernel.1), channel_id=1, replica_groups=mesh['xh'=2,'y'=4,'xl'=2,'z'=8,'c'=2] {'z'}, dimensions={0} | all-to-all | bytes 786432 | tf_op jit(solution)/shard_map/all_to_all | solution.py:23
  80.0 0.2 reroute_kernel.1
  80.2 14.3 %all_to_all.22.parts = bf16[32,16,128]{2,1,0:T(8,128)(2,1)S(1)} all-to-all(bf16[32,16,128]{2,1,0:T(8,128)(2,1)S(1)} %reroute_kernel.1), channel_id=1, replica_groups=mesh['xh'=2,'y'=4,'xl'=2,'z'=8,'c'=2] {'xh','y','xl','c'}, dimensions={0} | all-to-all | bytes 262144 | tf_op jit(solution)/shard_map/all_to_all | solution.py:23
  94.5 2.1 %update_kernel.1 = (f32[32,1024]{1,0:T(8,128)}, f32[32,448]{1,0:T(8,128)}, bf16[448,1024]{1,0:T(8,128)(2,1)}) custom-call(s32[4]{0:T(128)S(1)} %pad_add_fusion.place, bf16[32,16,128]{2,1,0:T(8,128)(2,1)S(1)} %all_to_all.22.parts, f32[32,1024]{1,0:T(8,128)S(1)} %copy-done, f32[32,448]{1,0:T(8,128)S(1)} %bitcast.13, bf16[448,1024]{1,0:T(8,128)(2,1)S(1)} %bitcast.10), custom_call_target="tpu_custom_call" | custom-call | tf_op jit(solution)/shard_map/update_kernel/pallas_call | solution.py:191
  (10 shorter events, 0.0 us)
Async XLA Ops:
  2.5 23.8 %all-to-all-start = ((bf16[16,32,512]{2,1,0:T(8,128)(2,1)}), bf16[16,32,512]{2,1,0:T(8,128)(2,1)S(1)}, u32[]{:S(2)}, u32[]{:S(2)}) async-start(bf16[16,32,512]{2,1,0:T(8,128)(2,1)} %get-tuple-element.19), calls=%async_computation | async-start | bytes 1048576 | tf_op jit(solution)/shard_map/all_to_all | solution.py:23
  12.5 4.8 %collective-permute-start = (bf16[32,1024]{1,0:T(8,128)(2,1)S(1)}, bf16[32,1024]{1,0:T(8,128)(2,1)S(1)}, u32[]{:S(2)}, u32[]{:S(2)}) collective-permute-start(bf16[32,1024]{1,0:T(8,128)(2,1)S(1)} %get-tuple-element.20), channel_id=1, source_target_pairs={{0,128},{128,0},{1,129},{129,1},{2,130},{130,2},{3,131},{131,3},{4... | collective-permute-start | bytes 196616 | tf_op jit(solution)/shard_map/ppermute | solution.py:204
  17.4 6.1 %collective-permute-start.3 = (bf16[2,32,1024]{2,1,0:T(8,128)(2,1)S(1)}, bf16[2,32,1024]{2,1,0:T(8,128)(2,1)S(1)}, u32[]{:S(2)}, u32[]{:S(2)}) collective-permute-start(bf16[2,32,1024]{2,1,0:T(8,128)(2,1)S(1)} %pad_maximum_fusion.down0), channel_id=1, source_target_pairs={{0,96},{32,64},{64,32},{96,0},{1,97},{33,65},{65,33},{97,1},{2,98}... | collective-permute-start | bytes 393224 | tf_op jit(solution)/shard_map/ppermute | solution.py:222
  20.2 5.5 %collective-permute-start.2 = (bf16[2,32,1024]{2,1,0:T(8,128)(2,1)S(1)}, bf16[2,32,1024]{2,1,0:T(8,128)(2,1)S(1)}, u32[]{:S(2)}, u32[]{:S(2)}) collective-permute-start(bf16[2,32,1024]{2,1,0:T(8,128)(2,1)S(1)} %pad_maximum_fusion.down0), channel_id=1, source_target_pairs={{0,64},{32,96},{64,0},{96,32},{1,65},{33,97},{65,1},{97,33},{2,66}... | collective-permute-start | bytes 393224 | tf_op jit(solution)/shard_map/ppermute | solution.py:222
  20.6 5.1 %collective-permute-start.1 = (bf16[2,32,1024]{2,1,0:T(8,128)(2,1)S(1)}, bf16[2,32,1024]{2,1,0:T(8,128)(2,1)S(1)}, u32[]{:S(2)}, u32[]{:S(2)}) collective-permute-start(bf16[2,32,1024]{2,1,0:T(8,128)(2,1)S(1)} %pad_maximum_fusion.down0), channel_id=1, source_target_pairs={{0,32},{32,0},{64,96},{96,64},{1,33},{33,1},{65,97},{97,65},{2,34}... | collective-permute-start | bytes 393224 | tf_op jit(solution)/shard_map/ppermute | solution.py:222
  26.3 10.0 %collective-permute-start.4 = (bf16[16,32,512]{2,1,0:T(8,128)(2,1)S(1)}, bf16[16,32,512]{2,1,0:T(8,128)(2,1)S(1)}, u32[]{:S(2)}, u32[]{:S(2)}) collective-permute-start(bf16[16,32,512]{2,1,0:T(8,128)(2,1)S(1)} %all-to-all-done.ups), channel_id=1, source_target_pairs={{0,1},{1,0},{2,3},{3,2},{4,5},{5,4},{6,7},{7,6},{8,9},{9,8},{10,11... | collective-permute-start | bytes 1572872 | tf_op jit(solution)/shard_map/ppermute | solution.py:204
  36.2 4.2 %collective-permute-start.6 = (bf16[16,14336]{1,0:T(8,128)(2,1)S(1)}, bf16[16,14336]{1,0:T(8,128)(2,1)S(1)}, u32[]{:S(2)}, u32[]{:S(2)}) collective-permute-start(bf16[16,14336]{1,0:T(8,128)(2,1)S(1)} %get-tuple-element.31), channel_id=1, source_target_pairs={{0,1},{1,0},{2,3},{3,2},{4,5},{5,4},{6,7},{7,6},{8,9},{9,8},{10,11... | collective-permute-start | bytes 1376264 | tf_op jit(solution)/shard_map/ppermute | solution.py:204
  36.3 24.4 %copy-start.2 = (f32[448,32]{0,1:T(8,128)S(1)}, f32[448,32]{0,1:T(8,128)}, u32[]{:S(2)}) copy-start(f32[448,32]{0,1:T(8,128)} %param.8) | copy-start | bytes 172036
  36.3 43.6 %copy-start = (f32[32,1024]{1,0:T(8,128)S(1)}, f32[32,1024]{1,0:T(8,128)}, u32[]{:S(2)}) copy-start(f32[32,1024]{1,0:T(8,128)} %factor_down.3) | copy-start | bytes 393220
  39.9 54.7 %copy-start.1 = (bf16[1024,448]{0,1:T(8,128)(2,1)S(1)}, bf16[1024,448]{0,1:T(8,128)(2,1)}, u32[]{:S(2)}) copy-start(bf16[1024,448]{0,1:T(8,128)(2,1)} %param.9) | copy-start | bytes 2752516
  39.9 1.7 %collective-permute-start.5 = (bf16[16,8192]{1,0:T(8,128)(2,1)S(1)}, bf16[16,8192]{1,0:T(8,128)(2,1)S(1)}, u32[]{:S(2)}, u32[]{:S(2)}) collective-permute-start(bf16[16,8192]{1,0:T(8,128)(2,1)S(1)} %get-tuple-element.29), channel_id=1, source_target_pairs={{0,1},{1,0},{2,3},{3,2},{4,5},{5,4},{6,7},{7,6},{8,9},{9,8},{10,11... | collective-permute-start | bytes 786440 | tf_op jit(solution)/shard_map/ppermute | solution.py:204

commit v5 on v4

--- a/solution.py
+++ b/solution.py
@@ -10,7 +10,7 @@
 norm_eps = 1e-06
 
 GRP = ("xh", "y")
-TP = ("xl", "z", "c")
+TP = ("xl", "zh", "zl", "c")
 PLANE = ("xh", "y", "xl")
 f32, bf16 = jnp.float32, jnp.bfloat16
 ALONG_LANES = (((1,), (1,)), ((), ()))
@@ -96,80 +96,93 @@
 
 
 def chip_sum_kernel(keep_a, got_a, keep_b, got_b, out, rows):
-    tile = 0
-    for keep, got in ((keep_a, got_a), (keep_b, got_b)):
-        for j in range(keep.shape[1] // 128):
-            columns = slice(128 * j, 128 * j + 128)
-            total = keep[:, columns].astype(f32) + got[:, columns].astype(f32)
-            for h in range(2):
-                rows[pl.ds(177 * 8 * h + tile, 8, 177), :] = total[8 * h : 8 * h + 8]
-            tile += 1
+    tiles = [(keep_a, got_a, 128 * j, j % 8 // 4, j // 8 * 4 + j % 4) for j in range(64)]
+    for j in range(112):
+        pair, k = divmod(j, 7)
+        odd = pair % 2
+        half = odd if k < 4 else 1 - odd
+        place = 32 + pair // 2 * 7 + (4 - half if odd else 0) + (k if k < 4 else k - 4)
+        tiles.append((keep_b, got_b, 128 * j, half, place))
+    for keep, got, start, half, place in tiles:
+        columns = slice(start, start + 128)
+        total = keep[:, columns].astype(f32) + got[:, columns].astype(f32)
+        for h in range(2):
+            rows[pl.ds(177 * 8 * h + 88 * half + place, 8, 177), :] = total[8 * h : 8 * h + 8]
     for r in range(16):
-        out[r] = rows[pl.ds(177 * r, 176), :].astype(bf16)
-
-
-def plane_sum_kernel(parts, factor_up, out, extra):
+        for half in range(2):
+            out[2 * r + half] = rows[pl.ds(177 * r + 88 * half, 88), :].astype(bf16)
+
+
+def plane_sum_kernel(parts, factor_up, out, rows):
     total = parts[0].astype(f32)
-    for k in range(1, 16):
+    for k in range(1, 32):
         total += parts[k].astype(f32)
     up = factor_up[...]
     line = jnp.full((1, 128), jnp.sum(up * up) * (1 / 8), f32)
     high = line.astype(bf16).astype(f32)
-    extra[...] = jnp.zeros((16, 128), f32)
-    extra[0:1] = high
-    extra[1:2] = line - high
-    block, last = total.astype(bf16), extra[...].astype(bf16)
-    for k in range(8):
-        out[k, :176] = block
-        out[k, 176:] = last
+    rows[0:88] = total
+    rows[88:96] = jnp.zeros((8, 128), f32)
+    rows[88:89] = high
+    rows[89:90] = line - high
+    block = rows[...].astype(bf16)
+    for k in range(4):
+        out[k] = block
 
 
 def reroute_kernel(parts, factor_down, out, row, rows):
     total = parts[0].astype(f32)
-    for k in range(1, 8):
+    for k in range(1, 4):
         total += parts[k].astype(f32)
-    grads = adapter_scale * total[:176]
+    grads = adapter_scale * total
     row[...] = grads
     squares = grads * grads
     down = factor_down[...]
     lane = lax.broadcasted_iota(jnp.int32, (1, 128), 1)
     line = jnp.where(
         lane < 64,
-        jnp.where(lane < 32, jnp.sum(squares[:64]), jnp.sum(squares[64:])),
-        jnp.where(lane < 96, jnp.sum(down * down) * (1 / 4), total[176:177] + total[177:178]),
+        jnp.where(lane < 32, jnp.sum(squares[:32]), jnp.sum(squares[32:88])),
+        jnp.where(lane < 96, jnp.sum(down * down) * (1 / 8), total[88:89] + total[89:90]),
     )
     high = line.astype(bf16).astype(f32)
     low = line - high
-    z = lax.axis_index("z")
+    pair = lax.axis_index("zh")
+    half = lax.axis_index("zl")
     for p in range(16):
-        for core in range(2):
-            k = 2 * p + core
-            rows[k, 0:8] = row[8 * (p // 2) : 8 * (p // 2) + 8]
-            rows[k, 8:12] = row[pl.ds(64 + 7 * (8 * (p % 2) + z) + 3 * core, 4), :]
-            rows[k, 12:13] = high
-            rows[k, 13:14] = low
-            rows[k, 14:16] = jnp.zeros((2, 128), f32)
-            out[k] = rows[k].astype(bf16)
+        for odd in range(2):
+            start = 32 + 7 * (4 * (p % 2) + pair) + (4 - half if odd else 0)
+            columns_b = row[pl.ds(start, 4), :]
+            for core in range(2):
+                k = 4 * p + 2 * odd + core
+                rows[k, 0:4] = row[4 * (p // 2) : 4 * (p // 2) + 4]
+                rows[k, 4:8] = columns_b
+                rows[k, 8:9] = high
+                rows[k, 9:10] = low
+                rows[k, 10:16] = jnp.zeros((6, 128), f32)
+                out[k] = rows[k].astype(bf16)
 
 
 def update_kernel(place, parts, factor_down, factor_up, base, new_down, new_up, merged, rows):
     line = jnp.zeros((1, 128), f32)
-    for k in range(32):
+    for k in range(64):
         block = parts[k].astype(f32)
         rows[pl.ds(k * 17, 16), :] = block
-        line += block[12:13] + block[13:14]
+        line += block[8:9] + block[9:10]
     scale_a = step_size * jnp.sqrt(line[:, 64:65]) / jnp.sqrt(line[:, 0:1] + norm_eps)
     scale_b = step_size * jnp.sqrt(line[:, 96:97]) / jnp.sqrt(line[:, 32:33] + norm_eps)
 
-    def ranks(j):
-        tiles = [rows[pl.ds(17 * core + 272 * h + j, 8, 34), :] for core in range(2) for h in range(2)]
-        return jnp.concatenate(tiles, 0)
+    def ranks(half, j):
+        starts = [34 * half + 17 * core + 544 * h + j for core in range(2) for h in range(2)]
+        return jnp.concatenate([rows[pl.ds(start, 8, 68), :] for start in starts], 0)
 
     for j in range(8):
         columns = slice(128 * j, 128 * j + 128)
-        new_down[:, columns] = factor_down[:, columns] - scale_a * ranks(j)
-    grad_b = jnp.concatenate([ranks(8 + j) for j in range(4)], 1)
-    grad_b = jnp.where(place[3] == 0, grad_b, pltpu.roll(grad_b, 448, 1))[:, :448]
+        new_down[:, columns] = factor_down[:, columns] - scale_a * ranks(j // 4, j % 4)
+    near, core = lax.axis_index("zl"), place[3]
+    tiles = [ranks(near, 4 + 3 * core)]
+    for j in range(1, 4):
+        tiles.append(ranks(jnp.where(core == 0, near, 1 - near), 4 + j - core))
+    grad_b = jnp.concatenate(tiles, 1)
+    grad_b = jnp.where(core == 0, grad_b, pltpu.roll(grad_b, 448, 1))[:, :448]
     new_up[...] = factor_up[...] - scale_b * grad_b
     left = new_up[...].T.astype(bf16)
     right = new_down[...].astype(bf16)
@@ -217,7 +230,7 @@
         in_hbm=(0, 1),
     )
     down_far = swap(down, "xh")
-    ups = exchange(up, ("xl", "z"))
+    ups = exchange(up, ("xl", "zh", "zl"))
     down0 = jnp.stack([down, down_far])
     downs = [down0] + [lax.ppermute(down0, "y", [(i, i ^ k) for i in range(4)]) for k in (1, 2, 3)]
     ups, downs = lax.optimization_barrier((ups, downs))
@@ -243,23 +256,21 @@
     )
     got_a = swap(give_a, "c")
     args = (keep_a, got_a, keep_b, got_b)
-    parts = kernel(chip_sum_kernel, shape((16, 176, 128), bf16), args, [pltpu.VMEM((2832, 128), f32)])
-    parts = exchange(parts, PLANE)
-    parts = kernel(
-        plane_sum_kernel, shape((8, 192, 128), bf16), (parts, factor_up), [pltpu.VMEM((16, 128), f32)]
-    )
-    parts = exchange(parts, "z")
-    scratch = [pltpu.VMEM((176, 128), f32), pltpu.VMEM((32, 16, 128), f32)]
-    parts = kernel(reroute_kernel, shape((32, 16, 128), bf16), (parts, factor_down), scratch)
-    parts = exchange(parts, PLANE + ("c",))
+    parts = kernel(chip_sum_kernel, shape((32, 88, 128), bf16), args, [pltpu.VMEM((3008, 128), f32)])
+    parts = exchange(parts, PLANE + ("zl",))
+    parts = kernel(plane_sum_kernel, shape((4, 96, 128), bf16), (parts, factor_up), [pltpu.VMEM((96, 128), f32)])
+    parts = exchange(parts, "zh")
+    scratch = [pltpu.VMEM((96, 128), f32), pltpu.VMEM((64, 16, 128), f32)]
+    parts = kernel(reroute_kernel, shape((64, 16, 128), bf16), (parts, factor_down), scratch)
+    parts = exchange(parts, PLANE + ("zl", "c"))
     outs = (shape((32, 1024), f32), shape((32, 448), f32), shape((448, 1024), bf16))
     args = (place, parts, factor_down, factor_up, base_weight.T)
-    new_down, new_up, merged = kernel(update_kernel, outs, args, [pltpu.VMEM((544, 128), f32)])
+    new_down, new_up, merged = kernel(update_kernel, outs, args, [pltpu.VMEM((1160, 128), f32)])
     return (new_down, new_up.T, merged.T)
 
 
 def solution(mesh):
-    fine = Mesh(mesh.devices.reshape(2, 4, 2, 8, 2), ("xh", "y", "xl", "z", "c"))
+    fine = Mesh(mesh.devices.reshape(2, 4, 2, 4, 2, 2), GRP + TP)
     return jax.shard_map(
         shards,
         mesh=fine,

time: 97 us -> 95.3 us (0.982)
  blocking collectives: 52.3 us -> 50.5 us
    all_to_all x3, blocking collectives: 52.3 us -> 50.5 us  [exchange(): return lax.all_to_all(x, axes, 0, 0, tiled=True)]
  transfers between devices with their start and end apart: 8 -> 8, of which waited for: 5 -> 5; matrix products, arithmetic and copies ran while one was open for 0% -> 0% of each run, Pallas kernels for 10% -> 11%
where the time goes in v5:
time: 95.3 us; the launch traced here: 95 us
  blocking collectives  50.5 us (53%)
  starting transfers between devices  20.1 us (21%)
  Pallas kernels  14.7 us (15%)
  waiting for transfers between devices  8.85 us (9%)
    all_to_all x3, blocking collectives, exchange(): return lax.all_to_all(x, axes, 0, 0, tiled=True)  50.5 us
    pallas_call x7, Pallas kernels, kernel(): pl.pallas_call(body, out_shape=outs, in_specs=specs, out_specs=jax.tree.m...  14.7 us
    all_to_all x1, starting transfers between devices, exchange(): return lax.all_to_all(x, axes, 0, 0, tiled=True)  10.1 us
    ppermute x4, starting transfers between devices, swap(): return lax.ppermute(x, axis, [(0, 1), (1, 0)])  6.56 us
    ppermute x3, waiting for transfers between devices, shards(): lax.ppermute(down0, 'y', [(i, i ^ k) for i in range(4)])  4.79 us
    ppermute x3, starting transfers between devices, shards(): lax.ppermute(down0, 'y', [(i, i ^ k) for i in range(4)])  3.5 us
    ppermute x4, waiting for transfers between devices, swap(): return lax.ppermute(x, axis, [(0, 1), (1, 0)])  3.45 us
  transfers between devices with their start and end apart: 8, of which 5 were waited for; matrix products, arithmetic and copies ran while one was open for 0% of the time, Pallas kernels for 11%

profile of v5, /device:TPU:1, one launch (start us, length us, event | category | flops | bytes accessed | tf_op | source)
XLA Modules:
  0.0 95.0 jit_solution(10006768498462072676)
XLA Ops:
  0.6 1.8 %prepare_kernel.1 = (bf16[32,1024]{1,0:T(8,128)(2,1)S(1)}, bf16[16,32,512]{2,1,0:T(8,128)(2,1)}) custom-call(f32[32,1024]{1,0:T(8,128)} %factor_down.3, f32[32,448]{1,0:T(8,128)} %bitcast.11), custom_call_target="tpu_custom_call" | custom-call | tf_op jit(solution)/shard_map/prepare_kernel/pallas_call | solution.py:204
  2.5 10.1 %all-to-all-start = ((bf16[16,32,512]{2,1,0:T(8,128)(2,1)}), bf16[16,32,512]{2,1,0:T(8,128)(2,1)S(1)}, u32[]{:S(2)}, u32[]{:S(2)}) async-start(bf16[16,32,512]{2,1,0:T(8,128)(2,1)} %get-tuple-element.19), calls=%async_computation | async-start | bytes 1048576 | tf_op jit(solution)/shard_map/all_to_all | solution.py:23
  12.5 2.5 %collective-permute-start = (bf16[32,1024]{1,0:T(8,128)(2,1)S(1)}, bf16[32,1024]{1,0:T(8,128)(2,1)S(1)}, u32[]{:S(2)}, u32[]{:S(2)}) collective-permute-start(bf16[32,1024]{1,0:T(8,128)(2,1)S(1)} %get-tuple-element.20), channel_id=1, source_target_pairs={{0,128},{128,0},{1,129},{129,1},{2,130},{130,2},{3,131},{131,3},{4... | collective-permute-start | bytes 196616 | tf_op jit(solution)/shard_map/ppermute | solution.py:217
  15.1 2.3 %collective-permute-done = bf16[32,1024]{1,0:T(8,128)(2,1)S(1)} collective-permute-done((bf16[32,1024]{1,0:T(8,128)(2,1)S(1)}, bf16[32,1024]{1,0:T(8,128)(2,1)S(1)}, u32[]{:S(2)}, u32[]{:S(2)}) %collective-permute-start) | collective-permute-done | bytes 65568 | tf_op jit(solution)/shard_map/ppermute | solution.py:217
  17.4 2.8 %collective-permute-start.3 = (bf16[2,32,1024]{2,1,0:T(8,128)(2,1)S(1)}, bf16[2,32,1024]{2,1,0:T(8,128)(2,1)S(1)}, u32[]{:S(2)}, u32[]{:S(2)}) collective-permute-start(bf16[2,32,1024]{2,1,0:T(8,128)(2,1)S(1)} %pad_maximum_fusion.down0), channel_id=1, source_target_pairs={{0,96},{32,64},{64,32},{96,0},{1,97},{33,65},{65,33},{97,1},{2,98}... | collective-permute-start | bytes 393224 | tf_op jit(solution)/shard_map/ppermute | solution.py:235
  20.2 0.3 collective-permute-start.2
  20.6 0.3 collective-permute-start.1
  20.9 2.6 %collective-permute-done.3.down3 = bf16[2,32,1024]{2,1,0:T(8,128)(2,1)S(1)} collective-permute-done((bf16[2,32,1024]{2,1,0:T(8,128)(2,1)S(1)}, bf16[2,32,1024]{2,1,0:T(8,128)(2,1)S(1)}, u32[]{:S(2)}, u32[]{:S(2)}) %collective-permute-start.3) | collective-permute-done | bytes 131104 | tf_op jit(solution)/shard_map/ppermute | solution.py:235
  23.5 2.1 %collective-permute-done.2.down2 = bf16[2,32,1024]{2,1,0:T(8,128)(2,1)S(1)} collective-permute-done((bf16[2,32,1024]{2,1,0:T(8,128)(2,1)S(1)}, bf16[2,32,1024]{2,1,0:T(8,128)(2,1)S(1)}, u32[]{:S(2)}, u32[]{:S(2)}) %collective-permute-start.2) | collective-permute-done | bytes 131104 | tf_op jit(solution)/shard_map/ppermute | solution.py:235
  25.7 0.6 all-to-all-done.ups
  26.3 3.4 %collective-permute-start.4 = (bf16[16,32,512]{2,1,0:T(8,128)(2,1)S(1)}, bf16[16,32,512]{2,1,0:T(8,128)(2,1)S(1)}, u32[]{:S(2)}, u32[]{:S(2)}) collective-permute-start(bf16[16,32,512]{2,1,0:T(8,128)(2,1)S(1)} %all-to-all-done.ups), channel_id=1, source_target_pairs={{0,1},{1,0},{2,3},{3,2},{4,5},{5,4},{6,7},{7,6},{8,9},{9,8},{10,11... | collective-permute-start | bytes 1572872 | tf_op jit(solution)/shard_map/ppermute | solution.py:217
  29.7 0.1 pad_add_fusion.place
  29.7 6.5 %grad_b_kernel.1 = (bf16[16,14336]{1,0:T(8,128)(2,1)S(1)}, bf16[16,14336]{1,0:T(8,128)(2,1)S(1)}, bf16[192,8192]{1,0:T(8,128)(2,1)S(1)}, bf16[192,14336]{1,0:T(8,128)(2,1)S(1)}) custom-call(s32[4]{0:T(128)S(1)} %pad_add_fusion.place, bf16[192,8192]{1,0:T(8,128)(2,1)} %tokens_hbm.1, bf16[192,14336]{1,0:T(8,128)(2,1)} %grads_hbm.1, ...), custom_call_target="tpu_custom_call" | custom-call | flops 300000000 | bytes 10485760 | tf_op jit(solution)/shard_map/grad_b_kernel/pallas_call | solution.py:204
  36.2 0.1 collective-permute-start.6
  36.4 3.5 %grad_a_kernel.1 = (bf16[16,8192]{1,0:T(8,128)(2,1)S(1)}, bf16[16,8192]{1,0:T(8,128)(2,1)S(1)}) custom-call(s32[4]{0:T(128)S(1)} %pad_add_fusion.place, bf16[192,8192]{1,0:T(8,128)(2,1)S(1)} %get-tuple-element.25.tokens, bf16[192,14336]{1,0:T(8,128)(2,1)S(1)} %get-tuple-element.26.grads, bf16[16,32,512]{2,1,0:T(8,128)(2,1)S(1)} %all-to-all-done.ups, ...), custom_call_target="tpu_custom_call" | custom-call | flops 300000000 | bytes 10485760 | tf_op jit(solution)/shard_map/grad_a_kernel/pallas_call | solution.py:204
  39.9 0.6 collective-permute-start.5
  40.4 1.2 %collective-permute-done.5.got_a = bf16[16,8192]{1,0:T(8,128)(2,1)S(1)} collective-permute-done((bf16[16,8192]{1,0:T(8,128)(2,1)S(1)}, bf16[16,8192]{1,0:T(8,128)(2,1)S(1)}, u32[]{:S(2)}, u32[]{:S(2)}) %collective-permute-start.5) | collective-permute-done | bytes 262176 | tf_op jit(solution)/shard_map/ppermute | solution.py:217
  41.6 0.2 chip_sum_kernel.1
  41.8 20.9 %all_to_all.20.parts = bf16[32,88,128]{2,1,0:T(8,128)(2,1)S(1)} all-to-all(bf16[32,88,128]{2,1,0:T(8,128)(2,1)S(1)} %chip_sum_kernel.1), channel_id=1, replica_groups=mesh['xh'=2,'y'=4,'xl'=2,'zh'=4,'zl'=2,'c'=2] {'xh','y','xl','zl'}, dimensions={0} | all-to-all | bytes 1441792 | tf_op jit(solution)/shard_map/all_to_all | solution.py:23
  62.7 0.2 plane_sum_kernel.1
  62.9 13.5 %all_to_all.21.parts = bf16[4,96,128]{2,1,0:T(8,128)(2,1)S(1)} all-to-all(bf16[4,96,128]{2,1,0:T(8,128)(2,1)S(1)} %plane_sum_kernel.1), channel_id=1, replica_groups=mesh['xh'=2,'y'=4,'xl'=2,'zh'=4,'zl'=2,'c'=2] {'zh'}, dimensions={0} | all-to-all | bytes 196608 | tf_op jit(solution)/shard_map/all_to_all | solution.py:23
  76.4 0.2 reroute_kernel.1
  76.6 16.2 %all_to_all.22.parts = bf16[64,16,128]{2,1,0:T(8,128)(2,1)S(1)} all-to-all(bf16[64,16,128]{2,1,0:T(8,128)(2,1)S(1)} %reroute_kernel.1), channel_id=1, replica_groups=mesh['xh'=2,'y'=4,'xl'=2,'zh'=4,'zl'=2,'c'=2] {'xh','y','xl','zl','c'}, dimensions={0} | all-to-all | bytes 524288 | tf_op jit(solution)/shard_map/all_to_all | solution.py:23
  92.8 2.2 %update_kernel.1 = (f32[32,1024]{1,0:T(8,128)}, f32[32,448]{1,0:T(8,128)}, bf16[448,1024]{1,0:T(8,128)(2,1)}) custom-call(s32[4]{0:T(128)S(1)} %pad_add_fusion.place, bf16[64,16,128]{2,1,0:T(8,128)(2,1)S(1)} %all_to_all.22.parts, f32[32,1024]{1,0:T(8,128)S(1)} %copy-done, f32[32,448]{1,0:T(8,128)S(1)} %bitcast.13, bf16[448,1024]{1,0:T(8,128)(2,1)S(1)} %bitcast.10), custom_call_target="tpu_custom_call" | custom-call | tf_op jit(solution)/shard_map/update_kernel/pallas_call | solution.py:204
  (10 shorter events, 0.0 us)
Async XLA Ops:
  2.5 23.8 %all-to-all-start = ((bf16[16,32,512]{2,1,0:T(8,128)(2,1)}), bf16[16,32,512]{2,1,0:T(8,128)(2,1)S(1)}, u32[]{:S(2)}, u32[]{:S(2)}) async-start(bf16[16,32,512]{2,1,0:T(8,128)(2,1)} %get-tuple-element.19), calls=%async_computation | async-start | bytes 1048576 | tf_op jit(solution)/shard_map/all_to_all | solution.py:23
  12.5 4.8 %collective-permute-start = (bf16[32,1024]{1,0:T(8,128)(2,1)S(1)}, bf16[32,1024]{1,0:T(8,128)(2,1)S(1)}, u32[]{:S(2)}, u32[]{:S(2)}) collective-permute-start(bf16[32,1024]{1,0:T(8,128)(2,1)S(1)} %get-tuple-element.20), channel_id=1, source_target_pairs={{0,128},{128,0},{1,129},{129,1},{2,130},{130,2},{3,131},{131,3},{4... | collective-permute-start | bytes 196616 | tf_op jit(solution)/shard_map/ppermute | solution.py:217
  17.4 6.1 %collective-permute-start.3 = (bf16[2,32,1024]{2,1,0:T(8,128)(2,1)S(1)}, bf16[2,32,1024]{2,1,0:T(8,128)(2,1)S(1)}, u32[]{:S(2)}, u32[]{:S(2)}) collective-permute-start(bf16[2,32,1024]{2,1,0:T(8,128)(2,1)S(1)} %pad_maximum_fusion.down0), channel_id=1, source_target_pairs={{0,96},{32,64},{64,32},{96,0},{1,97},{33,65},{65,33},{97,1},{2,98}... | collective-permute-start | bytes 393224 | tf_op jit(solution)/shard_map/ppermute | solution.py:235
  20.2 5.5 %collective-permute-start.2 = (bf16[2,32,1024]{2,1,0:T(8,128)(2,1)S(1)}, bf16[2,32,1024]{2,1,0:T(8,128)(2,1)S(1)}, u32[]{:S(2)}, u32[]{:S(2)}) collective-permute-start(bf16[2,32,1024]{2,1,0:T(8,128)(2,1)S(1)} %pad_maximum_fusion.down0), channel_id=1, source_target_pairs={{0,64},{32,96},{64,0},{96,32},{1,65},{33,97},{65,1},{97,33},{2,66}... | collective-permute-start | bytes 393224 | tf_op jit(solution)/shard_map/ppermute | solution.py:235
  20.6 5.1 %collective-permute-start.1 = (bf16[2,32,1024]{2,1,0:T(8,128)(2,1)S(1)}, bf16[2,32,1024]{2,1,0:T(8,128)(2,1)S(1)}, u32[]{:S(2)}, u32[]{:S(2)}) collective-permute-start(bf16[2,32,1024]{2,1,0:T(8,128)(2,1)S(1)} %pad_maximum_fusion.down0), channel_id=1, source_target_pairs={{0,32},{32,0},{64,96},{96,64},{1,33},{33,1},{65,97},{97,65},{2,34}... | collective-permute-start | bytes 393224 | tf_op jit(solution)/shard_map/ppermute | solution.py:235
  26.3 10.0 %collective-permute-start.4 = (bf16[16,32,512]{2,1,0:T(8,128)(2,1)S(1)}, bf16[16,32,512]{2,1,0:T(8,128)(2,1)S(1)}, u32[]{:S(2)}, u32[]{:S(2)}) collective-permute-start(bf16[16,32,512]{2,1,0:T(8,128)(2,1)S(1)} %all-to-all-done.ups), channel_id=1, source_target_pairs={{0,1},{1,0},{2,3},{3,2},{4,5},{5,4},{6,7},{7,6},{8,9},{9,8},{10,11... | collective-permute-start | bytes 1572872 | tf_op jit(solution)/shard_map/ppermute | solution.py:217
  36.2 4.2 %collective-permute-start.6 = (bf16[16,14336]{1,0:T(8,128)(2,1)S(1)}, bf16[16,14336]{1,0:T(8,128)(2,1)S(1)}, u32[]{:S(2)}, u32[]{:S(2)}) collective-permute-start(bf16[16,14336]{1,0:T(8,128)(2,1)S(1)} %get-tuple-element.31), channel_id=1, source_target_pairs={{0,1},{1,0},{2,3},{3,2},{4,5},{5,4},{6,7},{7,6},{8,9},{9,8},{10,11... | collective-permute-start | bytes 1376264 | tf_op jit(solution)/shard_map/ppermute | solution.py:217
  36.3 26.4 %copy-start.2 = (f32[448,32]{0,1:T(8,128)S(1)}, f32[448,32]{0,1:T(8,128)}, u32[]{:S(2)}) copy-start(f32[448,32]{0,1:T(8,128)} %param.8) | copy-start | bytes 172036
  36.3 40.1 %copy-start = (f32[32,1024]{1,0:T(8,128)S(1)}, f32[32,1024]{1,0:T(8,128)}, u32[]{:S(2)}) copy-start(f32[32,1024]{1,0:T(8,128)} %factor_down.3) | copy-start | bytes 393220
  36.3 56.5 %copy-start.1 = (bf16[1024,448]{0,1:T(8,128)(2,1)S(1)}, bf16[1024,448]{0,1:T(8,128)(2,1)}, u32[]{:S(2)}) copy-start(bf16[1024,448]{0,1:T(8,128)(2,1)} %param.9) | copy-start | bytes 2752516
  39.9 1.7 %collective-permute-start.5 = (bf16[16,8192]{1,0:T(8,128)(2,1)S(1)}, bf16[16,8192]{1,0:T(8,128)(2,1)S(1)}, u32[]{:S(2)}, u32[]{:S(2)}) collective-permute-start(bf16[16,8192]{1,0:T(8,128)(2,1)S(1)} %get-tuple-element.29), channel_id=1, source_target_pairs={{0,1},{1,0},{2,3},{3,2},{4,5},{5,4},{6,7},{7,6},{8,9},{9,8},{10,11... | collective-permute-start | bytes 786440 | tf_op jit(solution)/shard_map/ppermute | solution.py:217
